TPU v7x, 256 devices: a whole 4x4x8 slice. The times are simulated.
256 devices in a mesh: rep: 8 (over z), own: 32 (over x, y, core).
Axes of the slice: x: 4, y: 4, z: 8, core: 2. Of those that a mesh axis runs over, the one named last changes fastest.
Arguments:
- grads: bfloat16 [8, 192, 512, 512], P('rep', None, 'own'), may hold values from -6 to 6
- slot_of: int32 [192], P('rep'), may hold values from 0 to 31, as said below
- left_stats: float32 [8, 32, 512, 512], P('rep', 'own'), may hold values from -6 to 6
- right_stats: float32 [8, 32, 512, 512], P('rep', 'own'), may hold values from -6 to 6
- left_roots: bfloat16 [8, 32, 512, 512], P('rep', 'own'), may hold values from -0.25 to 0.25
- right_roots: bfloat16 [8, 32, 512, 512], P('rep', 'own'), may hold values from -0.25 to 0.25
Outputs:
- left_new: float32 [8, 32, 512, 512], P('rep', 'own')
- right_new: float32 [8, 32, 512, 512], P('rep', 'own')
- update: float32 [192, 512, 512], P('rep', 'own')
Inputs may be any that keep to these rules, and one draw needn't show every extreme that they name: `slot_of`: within each aligned run of 24 blocks (one group) the values are distinct; the value is the index along `own` of the device that keeps the block's statistics (each owner keeps exactly one slot); in every group 32 - 24 slots hold no block.
All inputs are finite; a program needn't handle non-finite values.
Results may differ from a plain program's by a relative error of at most 0.02.
Values may be sent and summed in bfloat16 or wider, within the bound.
No kernel may reach another device: no remote copies, remote signals or barrier semaphores. Data moves between devices by JAX's collectives and lax.ppermute only.
A program may use at most 128 MiB of HBM per device.

v0:
```python
import functools

import jax
import jax.numpy as jnp
from jax import lax
from jax.experimental import pallas as pl
from jax.experimental.pallas import tpu as pltpu
from jax.sharding import PartitionSpec as P

DECAY = 0.99
EPSILON = 1e-06
PARTS = 2
WAIT_BYTES = 20_000_000
VMEM = pl.BlockSpec(memory_space=pltpu.VMEM)
SMEM = pl.BlockSpec(memory_space=pltpu.SMEM)


def near(array):
    return pltpu.with_memory_space_constraint(array, pltpu.VMEM)


def ordered(first, second):
    return lax.optimization_barrier((first, second))


def add_kernel(got_ref, own_ref, out_ref, *, first, part):
    width = out_ref.shape[2]
    columns = pl.ds(part * width, width)
    blocks, got = out_ref.shape[0], got_ref.shape[0]
    if first > 0:
        out_ref[pl.ds(0, first)] = own_ref[pl.ds(0, first), :, columns]
    rows = pl.ds(first, got)
    out_ref[rows] = got_ref[...] + own_ref[rows, :, columns]
    rest = blocks - first - got
    if rest > 0:
        rows = pl.ds(first + got, rest)
        out_ref[rows] = own_ref[rows, :, columns]


def add(got, own, first, part):
    shape = own.shape[:2] + got.shape[2:]
    return pl.pallas_call(
        functools.partial(add_kernel, first=first, part=part),
        out_shape=jax.ShapeDtypeStruct(shape, got.dtype),
        in_specs=[VMEM] * 2,
        out_specs=VMEM,
        compiler_params=pltpu.CompilerParams(vmem_limit_bytes=4 << 20),
        cost_estimate=pl.CostEstimate(flops=0, bytes_accessed=WAIT_BYTES, transcendentals=0),
        name="add",
    )(near(got), near(own))


def chains(grads, replicas):
    me = lax.axis_index("rep")
    reach = replicas // 2
    groups = grads.reshape((replicas, -1) + grads.shape[1:])
    width = groups.shape[3] // PARTS
    ahead = [(i, (i + 1) % replicas) for i in range(replicas)]
    back = [(i, (i - 1) % replicas) for i in range(replicas)]

    def mine(group):
        return lax.dynamic_index_in_dim(groups, (group + replicas) % replicas, 0, False)

    def part_of(array, part):
        return array[:, :, part * width : (part + 1) * width]

    far, below, above = mine(me + reach), mine(me - reach + 1), mine(me + reach - 1)
    down = [lax.ppermute(part_of(far, 0), "rep", back), None]
    up = [None, lax.ppermute(part_of(far, 1), "rep", ahead)]
    down[1] = lax.ppermute(part_of(below, 1), "rep", back)
    up[0] = lax.ppermute(part_of(above, 0), "rep", ahead)
    last = None
    for step in range(reach - 1, 0, -1):
        for at, one, two in ((step, 0, 1), (step - 1, 1, 0)):
            if at == 0:
                continue
            for array, part, group, pairs in (
                (down, one, me - at, back),
                (up, two, me + at, ahead),
            ):
                got = array[part]
                if last is not None:
                    last, got = ordered(last, got)
                last = add(got, mine(group), 0, part)
                array[part] = lax.ppermute(last, "rep", pairs)
    return down, up, mine(me), last


def widen_kernel(own_ref, down_ref, out_ref, *, part):
    width = out_ref.shape[2]
    columns = pl.ds(part * width, width)
    out_ref[...] = down_ref[...].astype(jnp.float32) + own_ref[:, :, columns].astype(jnp.float32)


def widen(own, down, part):
    return pl.pallas_call(
        functools.partial(widen_kernel, part=part),
        out_shape=jax.ShapeDtypeStruct(down.shape, jnp.float32),
        in_specs=[VMEM] * 2,
        out_specs=VMEM,
        compiler_params=pltpu.CompilerParams(vmem_limit_bytes=4 << 20),
        cost_estimate=pl.CostEstimate(flops=0, bytes_accessed=WAIT_BYTES, transcendentals=0),
        name="widen",
    )(near(own), near(down))


def place_kernel(slot_ref, wide_ref, up_ref, *refs):
    before, out_ref = refs[:-1], refs[-1]
    width = up_ref.shape[2]
    here = pl.ds(out_ref.shape[2] - width, width)
    out_ref[:, :, here] = jnp.zeros((out_ref.shape[0],) + up_ref.shape[1:], out_ref.dtype)
    for ref in before:
        out_ref[:, :, pl.ds(0, ref.shape[2])] = ref[...]
    for b in range(up_ref.shape[0]):
        total = wide_ref[b] + up_ref[b].astype(jnp.float32)
        out_ref[slot_ref[b], :, here] = total.astype(out_ref.dtype)


def place(slot_of, wide, up, before, owners):
    strip, width = up.shape[1:]
    earlier = [] if before is None else [before]
    columns = width + sum(a.shape[2] for a in earlier)
    return pl.pallas_call(
        place_kernel,
        out_shape=jax.ShapeDtypeStruct((owners, strip, columns), up.dtype),
        in_specs=[SMEM] + [VMEM] * (2 + len(earlier)),
        out_specs=VMEM,
        compiler_params=pltpu.CompilerParams(vmem_limit_bytes=8 << 20),
        cost_estimate=pl.CostEstimate(flops=0, bytes_accessed=WAIT_BYTES, transcendentals=0),
        name="place",
    )(slot_of, near(wide), near(up), *[near(a) for a in earlier])


def step_kernel(block_ref, left_ref, right_ref, out_ref, precond_ref):
    size = block_ref.shape[0]
    tile = size // 4
    block = block_ref[...]
    squares = jnp.zeros((tile, size), jnp.float32)
    inputs = jnp.zeros((tile, size), jnp.float32)
    for i in range(4):
        rows = pl.ds(i * tile, tile)
        wide = block_ref[rows, :].astype(jnp.float32)
        inputs += wide * wide
        half = jnp.dot(left_ref[rows, :], block, preferred_element_type=jnp.float32)
        precond = jnp.dot(
            half.astype(jnp.bfloat16), right_ref[...], preferred_element_type=jnp.float32
        )
        precond_ref[rows, :] = precond
        squares += precond * precond
    count = 1.0 / (size * size)
    ratio = jnp.sqrt(jnp.sum(inputs, keepdims=True) * count + EPSILON) / jnp.sqrt(
        jnp.sum(squares, keepdims=True) * count + EPSILON
    )
    for i in range(4):
        rows = pl.ds(i * tile, tile)
        out_ref[rows, :] = (precond_ref[rows, :] * ratio).astype(out_ref.dtype)


def graft(block, left_root, right_root):
    size = block.shape[0]
    return pl.pallas_call(
        step_kernel,
        out_shape=jax.ShapeDtypeStruct(block.shape, block.dtype),
        in_specs=[VMEM] * 3,
        out_specs=VMEM,
        scratch_shapes=[pltpu.VMEM(block.shape, jnp.float32)],
        compiler_params=pltpu.CompilerParams(vmem_limit_bytes=8 << 20),
        cost_estimate=pl.CostEstimate(
            flops=4 * size**3, bytes_accessed=4 * block.size * 2, transcendentals=0
        ),
        name="graft",
    )(near(block), near(left_root), near(right_root))


def pick_kernel(slot_ref, rows_ref, out_ref):
    for b in range(out_ref.shape[0]):
        out_ref[b] = rows_ref[slot_ref[b]].astype(out_ref.dtype)


def pick(slot_of, rows):
    return pl.pallas_call(
        pick_kernel,
        out_shape=jax.ShapeDtypeStruct(slot_of.shape + rows.shape[1:], jnp.float32),
        in_specs=[SMEM, VMEM],
        out_specs=VMEM,
        compiler_params=pltpu.CompilerParams(vmem_limit_bytes=8 << 20),
        cost_estimate=pl.CostEstimate(flops=0, bytes_accessed=1_300_000, transcendentals=0),
        name="pick",
    )(slot_of, near(rows))


def local(grads, slot_of, left_stats, right_stats, left_roots, right_roots):
    replicas, owners = lax.axis_size("rep"), lax.axis_size("own")
    downs, ups, own, last = chains(grads[0], replicas)
    strip, width = own.shape[1:]
    block_size = strip * owners

    near_down, near_up = downs[1], ups[0]
    last, near_down = ordered(last, near_down)
    wide_last = widen(own, near_down, 1)
    wide_last, near_up = ordered(wide_last, near_up)
    wide_first = widen(own, near_up, 0)
    wide_first, far_down = ordered(wide_first, downs[0])
    sends = place(slot_of, wide_first, far_down, None, owners)
    sends, far_up = ordered(sends, ups[1])
    sends = place(slot_of, wide_last, far_up, sends, owners)
    block = lax.all_to_all(sends, "own", 0, 0, tiled=True).reshape(block_size, width)

    grafted = graft(block, left_roots[0, 0], right_roots[0, 0]).reshape(owners, strip, width)
    rows = lax.all_to_all(grafted, "own", 0, 0, tiled=True)

    gram_left = jnp.einsum("ik,jk->ij", block, block, preferred_element_type=jnp.float32)
    gram_right = jnp.einsum("ki,kj->ij", block, block, preferred_element_type=jnp.float32)
    left_next = DECAY * left_stats[0, 0] + (1.0 - DECAY) * gram_left
    right_next = DECAY * right_stats[0, 0] + (1.0 - DECAY) * gram_right

    update = pick(slot_of, rows)
    return left_next[None, None], right_next[None, None], update


def solution(mesh):
    return jax.shard_map(
        local,
        mesh=mesh,
        in_specs=(
            P("rep", None, "own", None),
            P("rep"),
            P("rep", "own", None, None),
            P("rep", "own", None, None),
            P("rep", "own", None, None),
            P("rep", "own", None, None),
        ),
        out_specs=(P("rep", "own", None, None), P("rep", "own", None, None), P("rep", "own", None)),
        check_vma=False,
    )
```

profile of v0, /device:TPU:1, one launch (start us, length us, event | category | flops | bytes accessed | tf_op | source)
XLA Modules:
  0.0 82.4 jit_solution(4745007587542166134)
XLA Ops:
  0.7 2.2 %dynamic-slice_bitcast_fusion = (bf16[24,16,512]{2,1,0:T(8,128)(2,1)S(1)}, bf16[24,16,512]{2,1,0:T(8,128)(2,1)S(1)}, bf16[24,16,512]{2,1,0:T(8,128)(2,1)S(1)}, b...) fusion(bf16[8,24,16,512]{3,2,1,0:T(8,128)(2,1)} %bitcast.45, ...), kind=kLoop, calls=%fused_computation.7 | loop fusion | bytes 6291488 | tf_op jit(solution)/shard_map/jit(dynamic_index_in_dim)/squeeze | solution.py:62
  2.9 6.5 %collective-permute-start = (bf16[24,16,256]{2,1,0:T(8,128)(2,1)S(1)}, bf16[24,16,256]{2,1,0:T(8,128)(2,1)S(1)}, u32[]{:S(2)}, u32[]{:S(2)}) collective-permute-start(bf16[24,16,256]{2,1,0:T(8,128)(2,1)S(1)} %get-tuple-element.44), channel_id=1, source_target_pairs={{0,224},{32,0},{64,32},{96,64},{128,96},{160,128},{192,160},{224,1... | collective-permute-start | bytes 589832 | tf_op jit(solution)/shard_map/ppermute | solution.py:68
  9.4 0.0 collective-permute-start.1
  9.4 2.7 %collective-permute-start.2 = (bf16[24,16,256]{2,1,0:T(8,128)(2,1)S(1)}, bf16[24,16,256]{2,1,0:T(8,128)(2,1)S(1)}, u32[]{:S(2)}, u32[]{:S(2)}) collective-permute-start(bf16[24,16,256]{2,1,0:T(8,128)(2,1)S(1)} %slice.18), channel_id=1, source_target_pairs={{0,224},{32,0},{64,32},{96,64},{128,96},{160,128},{192,160},{224,1... | collective-permute-start | bytes 589832 | tf_op jit(solution)/shard_map/ppermute | solution.py:70
  12.2 0.1 collective-permute-start.3
  12.3 0.7 collective-permute-done.got_ref
  13.0 3.5 %collective-permute-start.4 = (bf16[24,16,256]{2,1,0:T(8,128)(2,1)S(1)}, bf16[24,16,256]{2,1,0:T(8,128)(2,1)S(1)}, u32[]{:S(2)}, u32[]{:S(2)}) collective-permute-start(bf16[24,16,256]{2,1,0:T(8,128)(2,1)S(1)} %add.175), channel_id=1, source_target_pairs={{0,224},{32,0},{64,32},{96,64},{128,96},{160,128},{192,160},{224,1... | collective-permute-start | bytes 589832 | tf_op jit(solution)/shard_map/ppermute | solution.py:85
  16.5 0.0 collective-permute-done.1.got_ref
  16.5 0.1 collective-permute-start.5
  16.6 0.6 collective-permute-done.2.got_ref
  17.2 3.5 %collective-permute-start.6 = (bf16[24,16,256]{2,1,0:T(8,128)(2,1)S(1)}, bf16[24,16,256]{2,1,0:T(8,128)(2,1)S(1)}, u32[]{:S(2)}, u32[]{:S(2)}) collective-permute-start(bf16[24,16,256]{2,1,0:T(8,128)(2,1)S(1)} %add.177), channel_id=1, source_target_pairs={{0,224},{32,0},{64,32},{96,64},{128,96},{160,128},{192,160},{224,1... | collective-permute-start | bytes 589832 | tf_op jit(solution)/shard_map/ppermute | solution.py:85
  20.7 0.0 collective-permute-done.3.got_ref
  20.8 0.1 collective-permute-start.7
  20.9 0.0 collective-permute-done.4.got_ref
  20.9 0.0 copy-start.2
  20.9 3.3 %collective-permute-start.8 = (bf16[24,16,256]{2,1,0:T(8,128)(2,1)S(1)}, bf16[24,16,256]{2,1,0:T(8,128)(2,1)S(1)}, u32[]{:S(2)}, u32[]{:S(2)}) collective-permute-start(bf16[24,16,256]{2,1,0:T(8,128)(2,1)S(1)} %add.179), channel_id=1, source_target_pairs={{0,224},{32,0},{64,32},{96,64},{128,96},{160,128},{192,160},{224,1... | collective-permute-start | bytes 589832 | tf_op jit(solution)/shard_map/ppermute | solution.py:85
  24.2 0.0 collective-permute-done.5.got_ref
  24.3 0.1 collective-permute-start.9
  24.4 0.6 collective-permute-done.6.got_ref
  24.9 3.5 %collective-permute-start.10 = (bf16[24,16,256]{2,1,0:T(8,128)(2,1)S(1)}, bf16[24,16,256]{2,1,0:T(8,128)(2,1)S(1)}, u32[]{:S(2)}, u32[]{:S(2)}) collective-permute-start(bf16[24,16,256]{2,1,0:T(8,128)(2,1)S(1)} %add.181), channel_id=1, source_target_pairs={{0,224},{32,0},{64,32},{96,64},{128,96},{160,128},{192,160},{224,1... | collective-permute-start | bytes 589832 | tf_op jit(solution)/shard_map/ppermute | solution.py:85
  28.4 0.0 collective-permute-done.7.got_ref
  28.5 0.1 collective-permute-start.11
  28.6 0.3 collective-permute-done.8.got_ref
  28.9 0.0 copy-start
  28.9 0.0 copy-start.1
  29.0 3.5 %collective-permute-start.12 = (bf16[24,16,256]{2,1,0:T(8,128)(2,1)S(1)}, bf16[24,16,256]{2,1,0:T(8,128)(2,1)S(1)}, u32[]{:S(2)}, u32[]{:S(2)}) collective-permute-start(bf16[24,16,256]{2,1,0:T(8,128)(2,1)S(1)} %add.183), channel_id=1, source_target_pairs={{0,224},{32,0},{64,32},{96,64},{128,96},{160,128},{192,160},{224,1... | collective-permute-start | bytes 589832 | tf_op jit(solution)/shard_map/ppermute | solution.py:85
  32.5 0.0 collective-permute-done.9.got_ref
  32.5 0.1 collective-permute-start.13
  32.6 0.6 collective-permute-done.10.down_ref
  33.2 3.3 %collective-permute-done.11.down_ref = bf16[24,16,256]{2,1,0:T(8,128)(2,1)S(1)} collective-permute-done((bf16[24,16,256]{2,1,0:T(8,128)(2,1)S(1)}, bf16[24,16,256]{2,1,0:T(8,128)(2,1)S(1)}, u32[]{:S(2)}, u32[]{:S(2)}) %collective-permute-start.11) | collective-permute-done | bytes 196640 | tf_op jit(solution)/shard_map/ppermute | solution.py:85
  36.6 0.0 copy-start.3
  36.6 0.2 collective-permute-done.12.up_ref
  36.8 0.0 copy-done.2
  36.8 0.6 place.2.refs_0_
  37.4 2.7 %collective-permute-done.13.up_ref = bf16[24,16,256]{2,1,0:T(8,128)(2,1)S(1)} collective-permute-done((bf16[24,16,256]{2,1,0:T(8,128)(2,1)S(1)}, bf16[24,16,256]{2,1,0:T(8,128)(2,1)S(1)}, u32[]{:S(2)}, u32[]{:S(2)}) %collective-permute-start.13) | collective-permute-done | bytes 196640 | tf_op jit(solution)/shard_map/ppermute | solution.py:85
  40.1 0.6 place.3
  40.7 22.7 %all_to_all.10 = bf16[32,16,512]{2,1,0:T(8,128)(2,1)S(1)} all-to-all(bf16[32,16,512]{2,1,0:T(8,128)(2,1)S(1)} %place.3), channel_id=1, replica_groups=mesh['rep'=8,'own'=32] {'own'}, dimensions={0} | all-to-all | bytes 1048576 | tf_op jit(solution)/shard_map/all_to_all | solution.py:207
  63.4 0.0 copy-done
  63.4 0.0 copy-done.1
  63.4 0.0 copy-start.4
  63.4 2.2 %graft.1 = bf16[512,512]{1,0:T(8,128)(2,1)} custom-call(bf16[512,512]{1,0:T(8,128)(2,1)S(1)} %bitcast.41, bf16[512,512]{1,0:T(8,128)(2,1)S(1)} %bitcast.43, bf16[512,512]{1,0:T(8,128)(2,1)S(1)} %bitcast.44), custom_call_target="tpu_custom_call" | custom-call | flops 536870912 | bytes 2097152 | tf_op jit(solution)/shard_map/graft/pallas_call | solution.py:161
  65.6 3.7 %all-to-all-start.1 = ((bf16[32,16,512]{2,1,0:T(8,128)(2,1)}), bf16[32,16,512]{2,1,0:T(8,128)(2,1)S(1)}, u32[]{:S(2)}, u32[]{:S(2)}) async-start(bf16[32,16,512]{2,1,0:T(8,128)(2,1)} %bitcast.17), calls=%async_computation.1 | async-start | bytes 1048576 | tf_op jit(solution)/shard_map/all_to_all | solution.py:210
  69.3 0.0 copy-done.3
  69.3 1.4 %fusion.2 = f32[1,1,512,512]{3,2,1,0:T(8,128)} fusion(bf16[512,512]{1,0:T(8,128)(2,1)S(1)} %bitcast.42, f32[1,1,512,512]{3,2,1,0:T(8,128)S(1)} %copy-done.3), kind=kOutput, calls=%fused_computation.4 | convolution fusion | flops 269221888 | bytes 2621440 | tf_op jit(solution)/shard_map/ik,jk->ij/dot_general | solution.py:212
  70.8 0.0 copy-done.4
  70.8 1.5 %fusion.4 = f32[1,1,512,512]{3,2,1,0:T(8,128)} fusion(bf16[32,16,512]{2,1,0:T(8,128)(2,1)S(1)} %all_to_all.10, f32[1,1,512,512]{3,2,1,0:T(8,128)S(1)} %copy-done.4), kind=kOutput, calls=%fused_computation.6 | convolution fusion | flops 269221888 | bytes 2621440 | tf_op jit(solution)/shard_map/ki,kj->ij/dot_general | solution.py:213
  72.2 8.7 %all-to-all-done.1.rows_ref = bf16[32,16,512]{2,1,0:T(8,128)(2,1)S(1)} async-done(((bf16[32,16,512]{2,1,0:T(8,128)(2,1)}), bf16[32,16,512]{2,1,0:T(8,128)(2,1)S(1)}, u32[]{:S(2)}, u32[]{:S(2)}) %all-to-all-start.1) | async-done | bytes 524320 | tf_op jit(solution)/shard_map/all_to_all | solution.py:210
  80.9 1.5 %pick.1 = f32[24,16,512]{2,1,0:T(8,128)} custom-call(s32[24]{0:T(128)S(1)} %copy-done.2, bf16[32,16,512]{2,1,0:T(8,128)(2,1)S(1)} %all-to-all-done.1.rows_ref), custom_call_target="tpu_custom_call" | custom-call | bytes 1300000 | tf_op jit(solution)/shard_map/pick/pallas_call | solution.py:181
  (15 shorter events, 0.4 us)
Async XLA Ops:
  2.9 10.1 %collective-permute-start = (bf16[24,16,256]{2,1,0:T(8,128)(2,1)S(1)}, bf16[24,16,256]{2,1,0:T(8,128)(2,1)S(1)}, u32[]{:S(2)}, u32[]{:S(2)}) collective-permute-start(bf16[24,16,256]{2,1,0:T(8,128)(2,1)S(1)} %get-tuple-element.44), channel_id=1, source_target_pairs={{0,224},{32,0},{64,32},{96,64},{128,96},{160,128},{192,160},{224,1... | collective-permute-start | bytes 589832 | tf_op jit(solution)/shard_map/ppermute | solution.py:68
  9.4 7.1 %collective-permute-start.1 = (bf16[24,16,256]{2,1,0:T(8,128)(2,1)S(1)}, bf16[24,16,256]{2,1,0:T(8,128)(2,1)S(1)}, u32[]{:S(2)}, u32[]{:S(2)}) collective-permute-start(bf16[24,16,256]{2,1,0:T(8,128)(2,1)S(1)} %get-tuple-element.43), channel_id=1, source_target_pairs={{0,32},{32,64},{64,96},{96,128},{128,160},{160,192},{192,224},{224... | collective-permute-start | bytes 589832 | tf_op jit(solution)/shard_map/ppermute | solution.py:69
  9.4 7.8 %collective-permute-start.2 = (bf16[24,16,256]{2,1,0:T(8,128)(2,1)S(1)}, bf16[24,16,256]{2,1,0:T(8,128)(2,1)S(1)}, u32[]{:S(2)}, u32[]{:S(2)}) collective-permute-start(bf16[24,16,256]{2,1,0:T(8,128)(2,1)S(1)} %slice.18), channel_id=1, source_target_pairs={{0,224},{32,0},{64,32},{96,64},{128,96},{160,128},{192,160},{224,1... | collective-permute-start | bytes 589832 | tf_op jit(solution)/shard_map/ppermute | solution.py:70
  12.2 8.5 %collective-permute-start.3 = (bf16[24,16,256]{2,1,0:T(8,128)(2,1)S(1)}, bf16[24,16,256]{2,1,0:T(8,128)(2,1)S(1)}, u32[]{:S(2)}, u32[]{:S(2)}) collective-permute-start(bf16[24,16,256]{2,1,0:T(8,128)(2,1)S(1)} %slice.19), channel_id=1, source_target_pairs={{0,32},{32,64},{64,96},{96,128},{128,160},{160,192},{192,224},{224... | collective-permute-start | bytes 589832 | tf_op jit(solution)/shard_map/ppermute | solution.py:71
  13.0 7.8 %collective-permute-start.4 = (bf16[24,16,256]{2,1,0:T(8,128)(2,1)S(1)}, bf16[24,16,256]{2,1,0:T(8,128)(2,1)S(1)}, u32[]{:S(2)}, u32[]{:S(2)}) collective-permute-start(bf16[24,16,256]{2,1,0:T(8,128)(2,1)S(1)} %add.175), channel_id=1, source_target_pairs={{0,224},{32,0},{64,32},{96,64},{128,96},{160,128},{192,160},{224,1... | collective-permute-start | bytes 589832 | tf_op jit(solution)/shard_map/ppermute | solution.py:85
  16.5 7.7 %collective-permute-start.5 = (bf16[24,16,256]{2,1,0:T(8,128)(2,1)S(1)}, bf16[24,16,256]{2,1,0:T(8,128)(2,1)S(1)}, u32[]{:S(2)}, u32[]{:S(2)}) collective-permute-start(bf16[24,16,256]{2,1,0:T(8,128)(2,1)S(1)} %add.176), channel_id=1, source_target_pairs={{0,32},{32,64},{64,96},{96,128},{128,160},{160,192},{192,224},{224... | collective-permute-start | bytes 589832 | tf_op jit(solution)/shard_map/ppermute | solution.py:85
  17.2 7.7 %collective-permute-start.6 = (bf16[24,16,256]{2,1,0:T(8,128)(2,1)S(1)}, bf16[24,16,256]{2,1,0:T(8,128)(2,1)S(1)}, u32[]{:S(2)}, u32[]{:S(2)}) collective-permute-start(bf16[24,16,256]{2,1,0:T(8,128)(2,1)S(1)} %add.177), channel_id=1, source_target_pairs={{0,224},{32,0},{64,32},{96,64},{128,96},{160,128},{192,160},{224,1... | collective-permute-start | bytes 589832 | tf_op jit(solution)/shard_map/ppermute | solution.py:85
  20.8 7.7 %collective-permute-start.7 = (bf16[24,16,256]{2,1,0:T(8,128)(2,1)S(1)}, bf16[24,16,256]{2,1,0:T(8,128)(2,1)S(1)}, u32[]{:S(2)}, u32[]{:S(2)}) collective-permute-start(bf16[24,16,256]{2,1,0:T(8,128)(2,1)S(1)} %add.178), channel_id=1, source_target_pairs={{0,32},{32,64},{64,96},{96,128},{128,160},{160,192},{192,224},{224... | collective-permute-start | bytes 589832 | tf_op jit(solution)/shard_map/ppermute | solution.py:85
  20.9 15.9 %copy-start.2 = (s32[24]{0:T(128)S(1)}, s32[24]{0:T(128)}, u32[]{:S(2)}) copy-start(s32[24]{0:T(128)} %slot_ref.5) | copy-start | bytes 292
  20.9 8.0 %collective-permute-start.8 = (bf16[24,16,256]{2,1,0:T(8,128)(2,1)S(1)}, bf16[24,16,256]{2,1,0:T(8,128)(2,1)S(1)}, u32[]{:S(2)}, u32[]{:S(2)}) collective-permute-start(bf16[24,16,256]{2,1,0:T(8,128)(2,1)S(1)} %add.179), channel_id=1, source_target_pairs={{0,224},{32,0},{64,32},{96,64},{128,96},{160,128},{192,160},{224,1... | collective-permute-start | bytes 589832 | tf_op jit(solution)/shard_map/ppermute | solution.py:85
  24.3 8.2 %collective-permute-start.9 = (bf16[24,16,256]{2,1,0:T(8,128)(2,1)S(1)}, bf16[24,16,256]{2,1,0:T(8,128)(2,1)S(1)}, u32[]{:S(2)}, u32[]{:S(2)}) collective-permute-start(bf16[24,16,256]{2,1,0:T(8,128)(2,1)S(1)} %add.180), channel_id=1, source_target_pairs={{0,32},{32,64},{64,96},{96,128},{128,160},{160,192},{192,224},{224... | collective-permute-start | bytes 589832 | tf_op jit(solution)/shard_map/ppermute | solution.py:85
  24.9 8.2 %collective-permute-start.10 = (bf16[24,16,256]{2,1,0:T(8,128)(2,1)S(1)}, bf16[24,16,256]{2,1,0:T(8,128)(2,1)S(1)}, u32[]{:S(2)}, u32[]{:S(2)}) collective-permute-start(bf16[24,16,256]{2,1,0:T(8,128)(2,1)S(1)} %add.181), channel_id=1, source_target_pairs={{0,224},{32,0},{64,32},{96,64},{128,96},{160,128},{192,160},{224,1... | collective-permute-start | bytes 589832 | tf_op jit(solution)/shard_map/ppermute | solution.py:85
  28.5 8.1 %collective-permute-start.11 = (bf16[24,16,256]{2,1,0:T(8,128)(2,1)S(1)}, bf16[24,16,256]{2,1,0:T(8,128)(2,1)S(1)}, u32[]{:S(2)}, u32[]{:S(2)}) collective-permute-start(bf16[24,16,256]{2,1,0:T(8,128)(2,1)S(1)} %add.182), channel_id=1, source_target_pairs={{0,32},{32,64},{64,96},{96,128},{128,160},{160,192},{192,224},{224... | collective-permute-start | bytes 589832 | tf_op jit(solution)/shard_map/ppermute | solution.py:85
  28.9 34.5 %copy-start = (bf16[1,1,512,512]{3,2,1,0:T(8,128)(2,1)S(1)}, bf16[1,1,512,512]{3,2,1,0:T(8,128)(2,1)}, u32[]{:S(2)}) copy-start(bf16[1,1,512,512]{3,2,1,0:T(8,128)(2,1)} %param.10) | copy-start | bytes 1572868
  28.9 34.5 %copy-start.1 = (bf16[1,1,512,512]{3,2,1,0:T(8,128)(2,1)S(1)}, bf16[1,1,512,512]{3,2,1,0:T(8,128)(2,1)}, u32[]{:S(2)}) copy-start(bf16[1,1,512,512]{3,2,1,0:T(8,128)(2,1)} %param.11) | copy-start | bytes 1572868
  29.0 7.8 %collective-permute-start.12 = (bf16[24,16,256]{2,1,0:T(8,128)(2,1)S(1)}, bf16[24,16,256]{2,1,0:T(8,128)(2,1)S(1)}, u32[]{:S(2)}, u32[]{:S(2)}) collective-permute-start(bf16[24,16,256]{2,1,0:T(8,128)(2,1)S(1)} %add.183), channel_id=1, source_target_pairs={{0,224},{32,0},{64,32},{96,64},{128,96},{160,128},{192,160},{224,1... | collective-permute-start | bytes 589832 | tf_op jit(solution)/shard_map/ppermute | solution.py:85
  32.5 7.6 %collective-permute-start.13 = (bf16[24,16,256]{2,1,0:T(8,128)(2,1)S(1)}, bf16[24,16,256]{2,1,0:T(8,128)(2,1)S(1)}, u32[]{:S(2)}, u32[]{:S(2)}) collective-permute-start(bf16[24,16,256]{2,1,0:T(8,128)(2,1)S(1)} %add.184), channel_id=1, source_target_pairs={{0,32},{32,64},{64,96},{96,128},{128,160},{160,192},{192,224},{224... | collective-permute-start | bytes 589832 | tf_op jit(solution)/shard_map/ppermute | solution.py:85
  36.6 32.8 %copy-start.3 = (f32[1,1,512,512]{3,2,1,0:T(8,128)S(1)}, f32[1,1,512,512]{3,2,1,0:T(8,128)}, u32[]{:S(2)}) copy-start(f32[1,1,512,512]{3,2,1,0:T(8,128)} %param.8) | copy-start | bytes 3145732
  63.4 7.4 %copy-start.4 = (f32[1,1,512,512]{3,2,1,0:T(8,128)S(1)}, f32[1,1,512,512]{3,2,1,0:T(8,128)}, u32[]{:S(2)}) copy-start(f32[1,1,512,512]{3,2,1,0:T(8,128)} %param.9) | copy-start | bytes 3145732
  65.6 15.3 %all-to-all-start.1 = ((bf16[32,16,512]{2,1,0:T(8,128)(2,1)}), bf16[32,16,512]{2,1,0:T(8,128)(2,1)S(1)}, u32[]{:S(2)}, u32[]{:S(2)}) async-start(bf16[32,16,512]{2,1,0:T(8,128)(2,1)} %bitcast.17), calls=%async_computation.1 | async-start | bytes 1048576 | tf_op jit(solution)/shard_map/all_to_all | solution.py:210
where the time goes:
time: 82.6 us; the launch traced here: 82.4 us
  starting transfers between devices  30.7 us (37%)
  blocking collectives  22.7 us (27%)
  waiting for transfers between devices  17.7 us (21%)
  Pallas kernels  5.27 us (6%)
  matrix products  2.9 us (4%)
  local copies, waits for them, and re-layouts  2.25 us (3%)
  between operations  0.91 us (1%)
    all_to_all x1, blocking collectives, local(): lax.all_to_all(sends, 'own', 0, 0, tiled=True).reshape(block_size, width)  22.7 us
    ppermute x10, starting transfers between devices, chains(): array[part] = lax.ppermute(last, 'rep', pairs)  17.7 us
    all_to_all x1, waiting for transfers between devices, local(): rows = lax.all_to_all(grafted, 'own', 0, 0, tiled=True)  8.66 us
    ppermute x10, waiting for transfers between devices, chains(): array[part] = lax.ppermute(last, 'rep', pairs)  7.74 us
    ppermute x1, starting transfers between devices, chains(): down = [lax.ppermute(part_of(far, 0), 'rep', back), None]  6.48 us
    all_to_all x1, starting transfers between devices, local(): rows = lax.all_to_all(grafted, 'own', 0, 0, tiled=True)  3.68 us
    ppermute x1, starting transfers between devices, chains(): down[1] = lax.ppermute(part_of(below, 1), 'rep', back)  2.75 us
    pallas_call x1, Pallas kernels, graft(): pl.pallas_call(step_kernel, out_shape=jax.ShapeDtypeStruct(block.shape, b...  2.24 us
  transfers between devices with their start and end apart: 15, of which 9 were waited for; matrix products, arithmetic and copies ran while one was open for 4% of the time, Pallas kernels for 1%

commit v1 on v0

--- a/solution.py
+++ b/solution.py
@@ -64,9 +64,11 @@
     def part_of(array, part):
         return array[:, :, part * width : (part + 1) * width]
 
-    far, below, above = mine(me + reach), mine(me - reach + 1), mine(me + reach - 1)
+    far = mine(me + reach)
+    far, groups = ordered(far, groups)
     down = [lax.ppermute(part_of(far, 0), "rep", back), None]
     up = [None, lax.ppermute(part_of(far, 1), "rep", ahead)]
+    below, above = mine(me - reach + 1), mine(me + reach - 1)
     down[1] = lax.ppermute(part_of(below, 1), "rep", back)
     up[0] = lax.ppermute(part_of(above, 0), "rep", ahead)
     last = None
@@ -104,40 +106,52 @@
     )(near(own), near(down))
 
 
-def place_kernel(slot_ref, wide_ref, up_ref, *refs):
-    before, out_ref = refs[:-1], refs[-1]
-    width = up_ref.shape[2]
-    here = pl.ds(out_ref.shape[2] - width, width)
-    out_ref[:, :, here] = jnp.zeros((out_ref.shape[0],) + up_ref.shape[1:], out_ref.dtype)
-    for ref in before:
-        out_ref[:, :, pl.ds(0, ref.shape[2])] = ref[...]
-    for b in range(up_ref.shape[0]):
-        total = wide_ref[b] + up_ref[b].astype(jnp.float32)
-        out_ref[slot_ref[b], :, here] = total.astype(out_ref.dtype)
-
-
-def place(slot_of, wide, up, before, owners):
-    strip, width = up.shape[1:]
-    earlier = [] if before is None else [before]
-    columns = width + sum(a.shape[2] for a in earlier)
+def narrow_kernel(wide_ref, got_ref, out_ref):
+    out_ref[...] = (wide_ref[...] + got_ref[...].astype(jnp.float32)).astype(out_ref.dtype)
+
+
+def narrow(wide, got):
+    return pl.pallas_call(
+        narrow_kernel,
+        out_shape=jax.ShapeDtypeStruct(got.shape, got.dtype),
+        in_specs=[VMEM] * 2,
+        out_specs=VMEM,
+        compiler_params=pltpu.CompilerParams(vmem_limit_bytes=4 << 20),
+        cost_estimate=pl.CostEstimate(flops=0, bytes_accessed=WAIT_BYTES, transcendentals=0),
+        name="narrow",
+    )(near(wide), near(got))
+
+
+def place_kernel(slot_ref, first_ref, wide_ref, got_ref, out_ref):
+    width = got_ref.shape[2]
+    out_ref[...] = jnp.zeros_like(out_ref)
+    for b in range(got_ref.shape[0]):
+        slot = slot_ref[b]
+        total = wide_ref[b] + got_ref[b].astype(jnp.float32)
+        out_ref[slot, :, pl.ds(0, width)] = first_ref[b]
+        out_ref[slot, :, pl.ds(width, width)] = total.astype(out_ref.dtype)
+
+
+def place(slot_of, first, wide, got, owners):
+    strip, width = got.shape[1:]
     return pl.pallas_call(
         place_kernel,
-        out_shape=jax.ShapeDtypeStruct((owners, strip, columns), up.dtype),
-        in_specs=[SMEM] + [VMEM] * (2 + len(earlier)),
+        out_shape=jax.ShapeDtypeStruct((owners, strip, PARTS * width), got.dtype),
+        in_specs=[SMEM] + [VMEM] * 3,
         out_specs=VMEM,
         compiler_params=pltpu.CompilerParams(vmem_limit_bytes=8 << 20),
         cost_estimate=pl.CostEstimate(flops=0, bytes_accessed=WAIT_BYTES, transcendentals=0),
         name="place",
-    )(slot_of, near(wide), near(up), *[near(a) for a in earlier])
+    )(slot_of, near(first), near(wide), near(got))
 
 
 def step_kernel(block_ref, left_ref, right_ref, out_ref, precond_ref):
     size = block_ref.shape[0]
-    tile = size // 4
+    tile = size // 2
     block = block_ref[...]
     squares = jnp.zeros((tile, size), jnp.float32)
     inputs = jnp.zeros((tile, size), jnp.float32)
-    for i in range(4):
+    for i in range(2):
         rows = pl.ds(i * tile, tile)
         wide = block_ref[rows, :].astype(jnp.float32)
         inputs += wide * wide
@@ -151,7 +165,7 @@
     ratio = jnp.sqrt(jnp.sum(inputs, keepdims=True) * count + EPSILON) / jnp.sqrt(
         jnp.sum(squares, keepdims=True) * count + EPSILON
     )
-    for i in range(4):
+    for i in range(2):
         rows = pl.ds(i * tile, tile)
         out_ref[rows, :] = (precond_ref[rows, :] * ratio).astype(out_ref.dtype)
 
@@ -172,17 +186,29 @@
     )(near(block), near(left_root), near(right_root))
 
 
-def pick_kernel(slot_ref, rows_ref, out_ref):
-    for b in range(out_ref.shape[0]):
-        out_ref[b] = rows_ref[slot_ref[b]].astype(out_ref.dtype)
+def pick_kernel(slot_ref, rows_ref, out_ref, wide_ref, sems):
+    chunks = sems.shape[0]
+    count = wide_ref.shape[0] // chunks
+    copies = []
+    for chunk in range(chunks):
+        blocks = pl.ds(chunk * count, count)
+        for b in range(chunk * count, (chunk + 1) * count):
+            wide_ref[b] = rows_ref[slot_ref[b]].astype(wide_ref.dtype)
+        copy = pltpu.make_async_copy(wide_ref.at[blocks], out_ref.at[blocks], sems.at[chunk])
+        copy.start()
+        copies.append(copy)
+    for copy in copies:
+        copy.wait()
 
 
 def pick(slot_of, rows):
+    shape = slot_of.shape + rows.shape[1:]
     return pl.pallas_call(
         pick_kernel,
-        out_shape=jax.ShapeDtypeStruct(slot_of.shape + rows.shape[1:], jnp.float32),
+        out_shape=jax.ShapeDtypeStruct(shape, jnp.float32),
         in_specs=[SMEM, VMEM],
-        out_specs=VMEM,
+        out_specs=pl.BlockSpec(memory_space=pl.ANY),
+        scratch_shapes=[pltpu.VMEM(shape, jnp.float32), pltpu.SemaphoreType.DMA((4,))],
         compiler_params=pltpu.CompilerParams(vmem_limit_bytes=8 << 20),
         cost_estimate=pl.CostEstimate(flops=0, bytes_accessed=1_300_000, transcendentals=0),
         name="pick",
@@ -201,9 +227,8 @@
     wide_last, near_up = ordered(wide_last, near_up)
     wide_first = widen(own, near_up, 0)
     wide_first, far_down = ordered(wide_first, downs[0])
-    sends = place(slot_of, wide_first, far_down, None, owners)
-    sends, far_up = ordered(sends, ups[1])
-    sends = place(slot_of, wide_last, far_up, sends, owners)
+    first = narrow(wide_first, far_down)
+    sends = place(slot_of, first, wide_last, ups[1], owners)
     block = lax.all_to_all(sends, "own", 0, 0, tiled=True).reshape(block_size, width)
 
     grafted = graft(block, left_roots[0, 0], right_roots[0, 0]).reshape(owners, strip, width)

time: 82.6 us -> 81.7 us (0.989)
  starting transfers between devices: 30.7 us -> 29.4 us
  waiting for transfers between devices: 17.7 us -> 18.6 us
  local copies, waits for them, and re-layouts: 2.25 us -> 3.09 us
    ppermute x10, waiting for transfers between devices: 7.74 us -> 9.96 us  [chains(): array[part] = lax.ppermute(last, 'rep', pairs)]
    ppermute x10, starting transfers between devices: 17.7 us -> 16.4 us  [chains(): array[part] = lax.ppermute(last, 'rep', pairs)]
    squeeze x1 -> x2, local copies, waits for them, and re-layouts: 2.17 us -> 3.01 us  [mine(): lax.dynamic_index_in_dim(groups, (group + replicas) % replicas, 0, False)]
  transfers between devices with their start and end apart: 15 -> 15, of which waited for: 9 -> 8; matrix products, arithmetic and copies ran while one was open for 4% -> 6% of each run, Pallas kernels for 1% -> 1%
where the time goes in v1:
time: 81.7 us; the launch traced here: 81.4 us
  starting transfers between devices  29.4 us (36%)
  blocking collectives  22.1 us (27%)
  waiting for transfers between devices  18.6 us (23%)
  Pallas kernels  4.46 us (5%)
  local copies, waits for them, and re-layouts  3.09 us (4%)
  matrix products  2.9 us (4%)
  between operations  0.84 us (1%)
    all_to_all x1, blocking collectives, local(): lax.all_to_all(sends, 'own', 0, 0, tiled=True).reshape(block_size, width)  22.1 us
    ppermute x10, starting transfers between devices, chains(): array[part] = lax.ppermute(last, 'rep', pairs)  16.4 us
    ppermute x10, waiting for transfers between devices, chains(): array[part] = lax.ppermute(last, 'rep', pairs)  9.96 us
    all_to_all x1, waiting for transfers between devices, local(): rows = lax.all_to_all(grafted, 'own', 0, 0, tiled=True)  8.66 us
    ppermute x1, starting transfers between devices, chains(): down = [lax.ppermute(part_of(far, 0), 'rep', back), None]  6.48 us
    all_to_all x1, starting transfers between devices, local(): rows = lax.all_to_all(grafted, 'own', 0, 0, tiled=True)  3.68 us
    squeeze x2, local copies, waits for them, and re-layouts, mine(): lax.dynamic_index_in_dim(groups, (group + replicas) % replicas, 0, False)  3.01 us
    ppermute x1, starting transfers between devices, chains(): down[1] = lax.ppermute(part_of(below, 1), 'rep', back)  2.75 us
  transfers between devices with their start and end apart: 15, of which 8 were waited for; matrix products, arithmetic and copies ran while one was open for 6% of the time, Pallas kernels for 1%

profile of v1, /device:TPU:1, one launch (start us, length us, event | category | flops | bytes accessed | tf_op | source)
XLA Modules:
  0.0 81.4 jit_solution(3303973035468254052)
XLA Ops:
  0.6 1.0 %dynamic-slice_bitcast_fusion.7 = bf16[24,16,512]{2,1,0:T(8,128)(2,1)S(1)} fusion(bf16[8,24,16,512]{3,2,1,0:T(8,128)(2,1)} %bitcast.45, s32[]{:T(128)S(6)} %select_n.79), kind=kLoop, calls=%fused_computation.14 | loop fusion | bytes 786436 | tf_op jit(solution)/shard_map/jit(dynamic_index_in_dim)/squeeze | solution.py:62
  1.7 6.5 %collective-permute-start = (bf16[24,16,256]{2,1,0:T(8,128)(2,1)S(1)}, bf16[24,16,256]{2,1,0:T(8,128)(2,1)S(1)}, u32[]{:S(2)}, u32[]{:S(2)}) collective-permute-start(bf16[24,16,256]{2,1,0:T(8,128)(2,1)S(1)} %get-tuple-element.43), channel_id=1, source_target_pairs={{0,224},{32,0},{64,32},{96,64},{128,96},{160,128},{192,160},{224,1... | collective-permute-start | bytes 589832 | tf_op jit(solution)/shard_map/ppermute | solution.py:69
  8.2 0.0 collective-permute-start.1
  8.2 2.0 %dynamic-slice_bitcast_fusion = (bf16[24,16,512]{2,1,0:T(8,128)(2,1)S(1)}, bf16[24,16,512]{2,1,0:T(8,128)(2,1)S(1)}, bf16[24,16,512]{2,1,0:T(8,128)(2,1)S(1)}, b...) fusion(bf16[8,24,16,512]{3,2,1,0:T(8,128)(2,1)} %bitcast.46, ...), kind=kLoop, calls=%fused_computation.7 | loop fusion | bytes 5505052 | tf_op jit(solution)/shard_map/jit(dynamic_index_in_dim)/squeeze | solution.py:62
  10.2 2.8 %collective-permute-start.2 = (bf16[24,16,256]{2,1,0:T(8,128)(2,1)S(1)}, bf16[24,16,256]{2,1,0:T(8,128)(2,1)S(1)}, u32[]{:S(2)}, u32[]{:S(2)}) collective-permute-start(bf16[24,16,256]{2,1,0:T(8,128)(2,1)S(1)} %slice.16), channel_id=1, source_target_pairs={{0,224},{32,0},{64,32},{96,64},{128,96},{160,128},{192,160},{224,1... | collective-permute-start | bytes 589832 | tf_op jit(solution)/shard_map/ppermute | solution.py:72
  13.0 0.1 collective-permute-start.3
  13.1 0.0 collective-permute-done.got_ref
  13.1 2.7 %collective-permute-start.4 = (bf16[24,16,256]{2,1,0:T(8,128)(2,1)S(1)}, bf16[24,16,256]{2,1,0:T(8,128)(2,1)S(1)}, u32[]{:S(2)}, u32[]{:S(2)}) collective-permute-start(bf16[24,16,256]{2,1,0:T(8,128)(2,1)S(1)} %add.175), channel_id=1, source_target_pairs={{0,224},{32,0},{64,32},{96,64},{128,96},{160,128},{192,160},{224,1... | collective-permute-start | bytes 589832 | tf_op jit(solution)/shard_map/ppermute | solution.py:87
  15.8 0.0 collective-permute-done.1.got_ref
  15.9 0.1 collective-permute-start.5
  16.0 0.0 collective-permute-done.2.got_ref
  16.0 3.4 %collective-permute-start.6 = (bf16[24,16,256]{2,1,0:T(8,128)(2,1)S(1)}, bf16[24,16,256]{2,1,0:T(8,128)(2,1)S(1)}, u32[]{:S(2)}, u32[]{:S(2)}) collective-permute-start(bf16[24,16,256]{2,1,0:T(8,128)(2,1)S(1)} %add.177), channel_id=1, source_target_pairs={{0,224},{32,0},{64,32},{96,64},{128,96},{160,128},{192,160},{224,1... | collective-permute-start | bytes 589832 | tf_op jit(solution)/shard_map/ppermute | solution.py:87
  19.4 0.0 collective-permute-done.3.got_ref
  19.5 0.1 collective-permute-start.7
  19.6 1.0 %collective-permute-done.4.got_ref = bf16[24,16,256]{2,1,0:T(8,128)(2,1)S(1)} collective-permute-done((bf16[24,16,256]{2,1,0:T(8,128)(2,1)S(1)}, bf16[24,16,256]{2,1,0:T(8,128)(2,1)S(1)}, u32[]{:S(2)}, u32[]{:S(2)}) %collective-permute-start.4) | collective-permute-done | bytes 196640 | tf_op jit(solution)/shard_map/ppermute | solution.py:87
  20.6 3.5 %collective-permute-start.8 = (bf16[24,16,256]{2,1,0:T(8,128)(2,1)S(1)}, bf16[24,16,256]{2,1,0:T(8,128)(2,1)S(1)}, u32[]{:S(2)}, u32[]{:S(2)}) collective-permute-start(bf16[24,16,256]{2,1,0:T(8,128)(2,1)S(1)} %add.179), channel_id=1, source_target_pairs={{0,224},{32,0},{64,32},{96,64},{128,96},{160,128},{192,160},{224,1... | collective-permute-start | bytes 589832 | tf_op jit(solution)/shard_map/ppermute | solution.py:87
  24.1 0.0 collective-permute-done.5.got_ref
  24.1 0.0 copy-start.2
  24.1 0.1 collective-permute-start.9
  24.2 0.2 collective-permute-done.6.got_ref
  24.4 3.2 %collective-permute-start.10 = (bf16[24,16,256]{2,1,0:T(8,128)(2,1)S(1)}, bf16[24,16,256]{2,1,0:T(8,128)(2,1)S(1)}, u32[]{:S(2)}, u32[]{:S(2)}) collective-permute-start(bf16[24,16,256]{2,1,0:T(8,128)(2,1)S(1)} %add.181), channel_id=1, source_target_pairs={{0,224},{32,0},{64,32},{96,64},{128,96},{160,128},{192,160},{224,1... | collective-permute-start | bytes 589832 | tf_op jit(solution)/shard_map/ppermute | solution.py:87
  27.6 0.0 collective-permute-done.7.got_ref
  27.6 0.1 collective-permute-start.11
  27.7 0.9 %collective-permute-done.8.got_ref = bf16[24,16,256]{2,1,0:T(8,128)(2,1)S(1)} collective-permute-done((bf16[24,16,256]{2,1,0:T(8,128)(2,1)S(1)}, bf16[24,16,256]{2,1,0:T(8,128)(2,1)S(1)}, u32[]{:S(2)}, u32[]{:S(2)}) %collective-permute-start.8) | collective-permute-done | bytes 196640 | tf_op jit(solution)/shard_map/ppermute | solution.py:87
  28.6 0.0 copy-start
  28.6 0.0 copy-start.1
  28.7 3.2 %collective-permute-start.12 = (bf16[24,16,256]{2,1,0:T(8,128)(2,1)S(1)}, bf16[24,16,256]{2,1,0:T(8,128)(2,1)S(1)}, u32[]{:S(2)}, u32[]{:S(2)}) collective-permute-start(bf16[24,16,256]{2,1,0:T(8,128)(2,1)S(1)} %add.183), channel_id=1, source_target_pairs={{0,224},{32,0},{64,32},{96,64},{128,96},{160,128},{192,160},{224,1... | collective-permute-start | bytes 589832 | tf_op jit(solution)/shard_map/ppermute | solution.py:87
  31.8 0.0 collective-permute-done.9.got_ref
  31.8 0.1 collective-permute-start.13
  31.9 0.6 collective-permute-done.10.down_ref
  32.6 3.4 %collective-permute-done.11.down_ref = bf16[24,16,256]{2,1,0:T(8,128)(2,1)S(1)} collective-permute-done((bf16[24,16,256]{2,1,0:T(8,128)(2,1)S(1)}, bf16[24,16,256]{2,1,0:T(8,128)(2,1)S(1)}, u32[]{:S(2)}, u32[]{:S(2)}) %collective-permute-start.11) | collective-permute-done | bytes 196640 | tf_op jit(solution)/shard_map/ppermute | solution.py:87
  36.1 0.0 copy-start.3
  36.1 0.4 collective-permute-done.12.got_ref
  36.5 3.4 %collective-permute-done.13.got_ref = bf16[24,16,256]{2,1,0:T(8,128)(2,1)S(1)} collective-permute-done((bf16[24,16,256]{2,1,0:T(8,128)(2,1)S(1)}, bf16[24,16,256]{2,1,0:T(8,128)(2,1)S(1)}, u32[]{:S(2)}, u32[]{:S(2)}) %collective-permute-start.13) | collective-permute-done | bytes 196640 | tf_op jit(solution)/shard_map/ppermute | solution.py:87
  40.0 0.0 copy-done.2
  40.0 0.6 place.1
  40.6 22.1 %all_to_all.10 = bf16[32,16,512]{2,1,0:T(8,128)(2,1)S(1)} all-to-all(bf16[32,16,512]{2,1,0:T(8,128)(2,1)S(1)} %place.1), channel_id=1, replica_groups=mesh['rep'=8,'own'=32] {'own'}, dimensions={0} | all-to-all | bytes 1048576 | tf_op jit(solution)/shard_map/all_to_all | solution.py:232
  62.7 0.0 copy-done
  62.7 0.0 copy-done.1
  62.7 0.0 copy-start.4
  62.7 2.0 %graft.1 = bf16[512,512]{1,0:T(8,128)(2,1)} custom-call(bf16[512,512]{1,0:T(8,128)(2,1)S(1)} %bitcast.41, bf16[512,512]{1,0:T(8,128)(2,1)S(1)} %bitcast.43, bf16[512,512]{1,0:T(8,128)(2,1)S(1)} %bitcast.44), custom_call_target="tpu_custom_call" | custom-call | flops 536870912 | bytes 2097152 | tf_op jit(solution)/shard_map/graft/pallas_call | solution.py:175
  64.7 3.7 %all-to-all-start.1 = ((bf16[32,16,512]{2,1,0:T(8,128)(2,1)}), bf16[32,16,512]{2,1,0:T(8,128)(2,1)S(1)}, u32[]{:S(2)}, u32[]{:S(2)}) async-start(bf16[32,16,512]{2,1,0:T(8,128)(2,1)} %bitcast.17), calls=%async_computation.1 | async-start | bytes 1048576 | tf_op jit(solution)/shard_map/all_to_all | solution.py:235
  68.4 0.0 copy-done.3
  68.4 1.4 %fusion.2 = f32[1,1,512,512]{3,2,1,0:T(8,128)} fusion(bf16[512,512]{1,0:T(8,128)(2,1)S(1)} %bitcast.42, f32[1,1,512,512]{3,2,1,0:T(8,128)S(1)} %copy-done.3), kind=kOutput, calls=%fused_computation.4 | convolution fusion | flops 269221888 | bytes 2621440 | tf_op jit(solution)/shard_map/ik,jk->ij/dot_general | solution.py:237
  69.8 0.0 copy-done.4
  69.8 1.5 %fusion.4 = f32[1,1,512,512]{3,2,1,0:T(8,128)} fusion(bf16[32,16,512]{2,1,0:T(8,128)(2,1)S(1)} %all_to_all.10, f32[1,1,512,512]{3,2,1,0:T(8,128)S(1)} %copy-done.4), kind=kOutput, calls=%fused_computation.6 | convolution fusion | flops 269221888 | bytes 2621440 | tf_op jit(solution)/shard_map/ki,kj->ij/dot_general | solution.py:238
  71.3 8.7 %all-to-all-done.1.rows_ref = bf16[32,16,512]{2,1,0:T(8,128)(2,1)S(1)} async-done(((bf16[32,16,512]{2,1,0:T(8,128)(2,1)}), bf16[32,16,512]{2,1,0:T(8,128)(2,1)S(1)}, u32[]{:S(2)}, u32[]{:S(2)}) %all-to-all-start.1) | async-done | bytes 524320 | tf_op jit(solution)/shard_map/all_to_all | solution.py:235
  79.9 1.5 %pick.1 = f32[24,16,512]{2,1,0:T(8,128)} custom-call(s32[24]{0:T(128)S(1)} %copy-done.2, bf16[32,16,512]{2,1,0:T(8,128)(2,1)S(1)} %all-to-all-done.1.rows_ref), custom_call_target="tpu_custom_call" | custom-call | bytes 1300000 | tf_op jit(solution)/shard_map/pick/pallas_call | solution.py:206
  (16 shorter events, 0.5 us)
Async XLA Ops:
  1.7 11.4 %collective-permute-start = (bf16[24,16,256]{2,1,0:T(8,128)(2,1)S(1)}, bf16[24,16,256]{2,1,0:T(8,128)(2,1)S(1)}, u32[]{:S(2)}, u32[]{:S(2)}) collective-permute-start(bf16[24,16,256]{2,1,0:T(8,128)(2,1)S(1)} %get-tuple-element.43), channel_id=1, source_target_pairs={{0,224},{32,0},{64,32},{96,64},{128,96},{160,128},{192,160},{224,1... | collective-permute-start | bytes 589832 | tf_op jit(solution)/shard_map/ppermute | solution.py:69
  8.2 7.7 %collective-permute-start.1 = (bf16[24,16,256]{2,1,0:T(8,128)(2,1)S(1)}, bf16[24,16,256]{2,1,0:T(8,128)(2,1)S(1)}, u32[]{:S(2)}, u32[]{:S(2)}) collective-permute-start(bf16[24,16,256]{2,1,0:T(8,128)(2,1)S(1)} %get-tuple-element.42), channel_id=1, source_target_pairs={{0,32},{32,64},{64,96},{96,128},{128,160},{160,192},{192,224},{224... | collective-permute-start | bytes 589832 | tf_op jit(solution)/shard_map/ppermute | solution.py:70
  10.2 5.8 %collective-permute-start.2 = (bf16[24,16,256]{2,1,0:T(8,128)(2,1)S(1)}, bf16[24,16,256]{2,1,0:T(8,128)(2,1)S(1)}, u32[]{:S(2)}, u32[]{:S(2)}) collective-permute-start(bf16[24,16,256]{2,1,0:T(8,128)(2,1)S(1)} %slice.16), channel_id=1, source_target_pairs={{0,224},{32,0},{64,32},{96,64},{128,96},{160,128},{192,160},{224,1... | collective-permute-start | bytes 589832 | tf_op jit(solution)/shard_map/ppermute | solution.py:72
  13.0 6.5 %collective-permute-start.3 = (bf16[24,16,256]{2,1,0:T(8,128)(2,1)S(1)}, bf16[24,16,256]{2,1,0:T(8,128)(2,1)S(1)}, u32[]{:S(2)}, u32[]{:S(2)}) collective-permute-start(bf16[24,16,256]{2,1,0:T(8,128)(2,1)S(1)} %slice.17), channel_id=1, source_target_pairs={{0,32},{32,64},{64,96},{96,128},{128,160},{160,192},{192,224},{224... | collective-permute-start | bytes 589832 | tf_op jit(solution)/shard_map/ppermute | solution.py:73
  13.1 7.5 %collective-permute-start.4 = (bf16[24,16,256]{2,1,0:T(8,128)(2,1)S(1)}, bf16[24,16,256]{2,1,0:T(8,128)(2,1)S(1)}, u32[]{:S(2)}, u32[]{:S(2)}) collective-permute-start(bf16[24,16,256]{2,1,0:T(8,128)(2,1)S(1)} %add.175), channel_id=1, source_target_pairs={{0,224},{32,0},{64,32},{96,64},{128,96},{160,128},{192,160},{224,1... | collective-permute-start | bytes 589832 | tf_op jit(solution)/shard_map/ppermute | solution.py:87
  15.9 8.2 %collective-permute-start.5 = (bf16[24,16,256]{2,1,0:T(8,128)(2,1)S(1)}, bf16[24,16,256]{2,1,0:T(8,128)(2,1)S(1)}, u32[]{:S(2)}, u32[]{:S(2)}) collective-permute-start(bf16[24,16,256]{2,1,0:T(8,128)(2,1)S(1)} %add.176), channel_id=1, source_target_pairs={{0,32},{32,64},{64,96},{96,128},{128,160},{160,192},{192,224},{224... | collective-permute-start | bytes 589832 | tf_op jit(solution)/shard_map/ppermute | solution.py:87
  16.0 8.4 %collective-permute-start.6 = (bf16[24,16,256]{2,1,0:T(8,128)(2,1)S(1)}, bf16[24,16,256]{2,1,0:T(8,128)(2,1)S(1)}, u32[]{:S(2)}, u32[]{:S(2)}) collective-permute-start(bf16[24,16,256]{2,1,0:T(8,128)(2,1)S(1)} %add.177), channel_id=1, source_target_pairs={{0,224},{32,0},{64,32},{96,64},{128,96},{160,128},{192,160},{224,1... | collective-permute-start | bytes 589832 | tf_op jit(solution)/shard_map/ppermute | solution.py:87
  19.5 8.1 %collective-permute-start.7 = (bf16[24,16,256]{2,1,0:T(8,128)(2,1)S(1)}, bf16[24,16,256]{2,1,0:T(8,128)(2,1)S(1)}, u32[]{:S(2)}, u32[]{:S(2)}) collective-permute-start(bf16[24,16,256]{2,1,0:T(8,128)(2,1)S(1)} %add.178), channel_id=1, source_target_pairs={{0,32},{32,64},{64,96},{96,128},{128,160},{160,192},{192,224},{224... | collective-permute-start | bytes 589832 | tf_op jit(solution)/shard_map/ppermute | solution.py:87
  20.6 8.0 %collective-permute-start.8 = (bf16[24,16,256]{2,1,0:T(8,128)(2,1)S(1)}, bf16[24,16,256]{2,1,0:T(8,128)(2,1)S(1)}, u32[]{:S(2)}, u32[]{:S(2)}) collective-permute-start(bf16[24,16,256]{2,1,0:T(8,128)(2,1)S(1)} %add.179), channel_id=1, source_target_pairs={{0,224},{32,0},{64,32},{96,64},{128,96},{160,128},{192,160},{224,1... | collective-permute-start | bytes 589832 | tf_op jit(solution)/shard_map/ppermute | solution.py:87
  24.1 15.8 %copy-start.2 = (s32[24]{0:T(128)S(1)}, s32[24]{0:T(128)}, u32[]{:S(2)}) copy-start(s32[24]{0:T(128)} %slot_ref.3) | copy-start | bytes 292
  24.1 7.7 %collective-permute-start.9 = (bf16[24,16,256]{2,1,0:T(8,128)(2,1)S(1)}, bf16[24,16,256]{2,1,0:T(8,128)(2,1)S(1)}, u32[]{:S(2)}, u32[]{:S(2)}) collective-permute-start(bf16[24,16,256]{2,1,0:T(8,128)(2,1)S(1)} %add.180), channel_id=1, source_target_pairs={{0,32},{32,64},{64,96},{96,128},{128,160},{160,192},{192,224},{224... | collective-permute-start | bytes 589832 | tf_op jit(solution)/shard_map/ppermute | solution.py:87
  24.4 8.1 %collective-permute-start.10 = (bf16[24,16,256]{2,1,0:T(8,128)(2,1)S(1)}, bf16[24,16,256]{2,1,0:T(8,128)(2,1)S(1)}, u32[]{:S(2)}, u32[]{:S(2)}) collective-permute-start(bf16[24,16,256]{2,1,0:T(8,128)(2,1)S(1)} %add.181), channel_id=1, source_target_pairs={{0,224},{32,0},{64,32},{96,64},{128,96},{160,128},{192,160},{224,1... | collective-permute-start | bytes 589832 | tf_op jit(solution)/shard_map/ppermute | solution.py:87
  27.6 8.4 %collective-permute-start.11 = (bf16[24,16,256]{2,1,0:T(8,128)(2,1)S(1)}, bf16[24,16,256]{2,1,0:T(8,128)(2,1)S(1)}, u32[]{:S(2)}, u32[]{:S(2)}) collective-permute-start(bf16[24,16,256]{2,1,0:T(8,128)(2,1)S(1)} %add.182), channel_id=1, source_target_pairs={{0,32},{32,64},{64,96},{96,128},{128,160},{160,192},{192,224},{224... | collective-permute-start | bytes 589832 | tf_op jit(solution)/shard_map/ppermute | solution.py:87
  28.6 34.1 %copy-start = (bf16[1,1,512,512]{3,2,1,0:T(8,128)(2,1)S(1)}, bf16[1,1,512,512]{3,2,1,0:T(8,128)(2,1)}, u32[]{:S(2)}) copy-start(bf16[1,1,512,512]{3,2,1,0:T(8,128)(2,1)} %param.10) | copy-start | bytes 1572868
  28.6 34.0 %copy-start.1 = (bf16[1,1,512,512]{3,2,1,0:T(8,128)(2,1)S(1)}, bf16[1,1,512,512]{3,2,1,0:T(8,128)(2,1)}, u32[]{:S(2)}) copy-start(bf16[1,1,512,512]{3,2,1,0:T(8,128)(2,1)} %param.11) | copy-start | bytes 1572868
  28.7 7.8 %collective-permute-start.12 = (bf16[24,16,256]{2,1,0:T(8,128)(2,1)S(1)}, bf16[24,16,256]{2,1,0:T(8,128)(2,1)S(1)}, u32[]{:S(2)}, u32[]{:S(2)}) collective-permute-start(bf16[24,16,256]{2,1,0:T(8,128)(2,1)S(1)} %add.183), channel_id=1, source_target_pairs={{0,224},{32,0},{64,32},{96,64},{128,96},{160,128},{192,160},{224,1... | collective-permute-start | bytes 589832 | tf_op jit(solution)/shard_map/ppermute | solution.py:87
  31.8 8.1 %collective-permute-start.13 = (bf16[24,16,256]{2,1,0:T(8,128)(2,1)S(1)}, bf16[24,16,256]{2,1,0:T(8,128)(2,1)S(1)}, u32[]{:S(2)}, u32[]{:S(2)}) collective-permute-start(bf16[24,16,256]{2,1,0:T(8,128)(2,1)S(1)} %add.184), channel_id=1, source_target_pairs={{0,32},{32,64},{64,96},{96,128},{128,160},{160,192},{192,224},{224... | collective-permute-start | bytes 589832 | tf_op jit(solution)/shard_map/ppermute | solution.py:87
  36.1 32.3 %copy-start.3 = (f32[1,1,512,512]{3,2,1,0:T(8,128)S(1)}, f32[1,1,512,512]{3,2,1,0:T(8,128)}, u32[]{:S(2)}) copy-start(f32[1,1,512,512]{3,2,1,0:T(8,128)} %param.8) | copy-start | bytes 3145732
  62.7 7.1 %copy-start.4 = (f32[1,1,512,512]{3,2,1,0:T(8,128)S(1)}, f32[1,1,512,512]{3,2,1,0:T(8,128)}, u32[]{:S(2)}) copy-start(f32[1,1,512,512]{3,2,1,0:T(8,128)} %param.9) | copy-start | bytes 3145732
  64.7 15.3 %all-to-all-start.1 = ((bf16[32,16,512]{2,1,0:T(8,128)(2,1)}), bf16[32,16,512]{2,1,0:T(8,128)(2,1)S(1)}, u32[]{:S(2)}, u32[]{:S(2)}) async-start(bf16[32,16,512]{2,1,0:T(8,128)(2,1)} %bitcast.17), calls=%async_computation.1 | async-start | bytes 1048576 | tf_op jit(solution)/shard_map/all_to_all | solution.py:235

commit v2 on v0

--- a/solution.py
+++ b/solution.py
@@ -12,7 +12,6 @@
 PARTS = 2
 WAIT_BYTES = 20_000_000
 VMEM = pl.BlockSpec(memory_space=pltpu.VMEM)
-SMEM = pl.BlockSpec(memory_space=pltpu.SMEM)
 
 
 def near(array):
@@ -21,6 +20,34 @@
 
 def ordered(first, second):
     return lax.optimization_barrier((first, second))
+
+
+def slice_kernel(groups_ref, one_ref, two_ref, sems, *, picks):
+    me = lax.axis_index("rep")
+    width = one_ref.shape[2]
+    copies = []
+    for at, (out_ref, (ahead, part)) in enumerate(zip((one_ref, two_ref), picks)):
+        group = lax.rem(me + ahead, groups_ref.shape[0])
+        source = groups_ref.at[group, :, :, pl.ds(part * width, width)]
+        copies.append(pltpu.make_async_copy(source, out_ref, sems.at[at]))
+    for copy in copies:
+        copy.start()
+    for copy in copies:
+        copy.wait()
+
+
+def slices(groups, picks):
+    shape = groups.shape[1:3] + (groups.shape[3] // PARTS,)
+    return pl.pallas_call(
+        functools.partial(slice_kernel, picks=picks),
+        out_shape=[jax.ShapeDtypeStruct(shape, groups.dtype)] * 2,
+        in_specs=[pl.BlockSpec(memory_space=pltpu.HBM)],
+        out_specs=[VMEM] * 2,
+        scratch_shapes=[pltpu.SemaphoreType.DMA((2,))],
+        compiler_params=pltpu.CompilerParams(vmem_limit_bytes=4 << 20),
+        cost_estimate=pl.CostEstimate(flops=0, bytes_accessed=1_000_000, transcendentals=0),
+        name="slices",
+    )(pltpu.with_memory_space_constraint(groups, pltpu.HBM))
 
 
 def add_kernel(got_ref, own_ref, out_ref, *, first, part):
@@ -50,40 +77,40 @@
     )(near(got), near(own))
 
 
-def chains(grads, replicas):
+def chains(grads, replicas, chosen):
     me = lax.axis_index("rep")
     reach = replicas // 2
     groups = grads.reshape((replicas, -1) + grads.shape[1:])
-    width = groups.shape[3] // PARTS
-    ahead = [(i, (i + 1) % replicas) for i in range(replicas)]
-    back = [(i, (i - 1) % replicas) for i in range(replicas)]
+    ahead = [(i, (i - 1) % replicas) for i in range(replicas)]
+    back = [(i, (i + 1) % replicas) for i in range(replicas)]
 
     def mine(group):
         return lax.dynamic_index_in_dim(groups, (group + replicas) % replicas, 0, False)
 
-    def part_of(array, part):
-        return array[:, :, part * width : (part + 1) * width]
-
-    far, below, above = mine(me + reach), mine(me - reach + 1), mine(me + reach - 1)
-    down = [lax.ppermute(part_of(far, 0), "rep", back), None]
-    up = [None, lax.ppermute(part_of(far, 1), "rep", ahead)]
-    down[1] = lax.ppermute(part_of(below, 1), "rep", back)
-    up[0] = lax.ppermute(part_of(above, 0), "rep", ahead)
+    down, up = [None, None], [None, None]
+    one, two = slices(groups, ((reach, 0), (reach, 1)))
+    down[0], up[1] = lax.ppermute(one, "rep", back), lax.ppermute(two, "rep", ahead)
+    one, groups = ordered(one, groups)
+    one, two = slices(groups, ((reach - 1, 1), (reach + 1, 0)))
+    down[1], up[0] = lax.ppermute(one, "rep", back), lax.ppermute(two, "rep", ahead)
+    one, groups = ordered(one, groups)
     last = None
     for step in range(reach - 1, 0, -1):
         for at, one, two in ((step, 0, 1), (step - 1, 1, 0)):
             if at == 0:
                 continue
             for array, part, group, pairs in (
-                (down, one, me - at, back),
-                (up, two, me + at, ahead),
+                (down, one, me + at, back),
+                (up, two, me - at, ahead),
             ):
                 got = array[part]
                 if last is not None:
                     last, got = ordered(last, got)
+                if step == reach - 2 and not at == step:
+                    chosen, got = ordered(chosen, got)
                 last = add(got, mine(group), 0, part)
                 array[part] = lax.ppermute(last, "rep", pairs)
-    return down, up, mine(me), last
+    return down, up, mine(me), last, chosen
 
 
 def widen_kernel(own_ref, down_ref, out_ref, *, part):
@@ -104,40 +131,49 @@
     )(near(own), near(down))
 
 
-def place_kernel(slot_ref, wide_ref, up_ref, *refs):
+def selections(slot_of, owners, strip):
+    slot = jnp.repeat(slot_of, strip)
+    blocks, slots = jnp.arange(slot.shape[0]), jnp.arange(owners * strip)
+    same_row = blocks[None, :] % strip == slots[:, None] % strip
+    put = (slot[None, :] == slots[:, None] // strip) & same_row
+    take = (slot[:, None] == slots[None, :] // strip) & (
+        blocks[:, None] % strip == slots[None, :] % strip
+    )
+    return put.astype(jnp.bfloat16), take.astype(jnp.bfloat16)
+
+
+def place_kernel(put_ref, wide_ref, got_ref, *refs):
     before, out_ref = refs[:-1], refs[-1]
-    width = up_ref.shape[2]
-    here = pl.ds(out_ref.shape[2] - width, width)
-    out_ref[:, :, here] = jnp.zeros((out_ref.shape[0],) + up_ref.shape[1:], out_ref.dtype)
+    width = got_ref.shape[2]
+    total = (wide_ref[...] + got_ref[...].astype(jnp.float32)).astype(out_ref.dtype)
     for ref in before:
-        out_ref[:, :, pl.ds(0, ref.shape[2])] = ref[...]
-    for b in range(up_ref.shape[0]):
-        total = wide_ref[b] + up_ref[b].astype(jnp.float32)
-        out_ref[slot_ref[b], :, here] = total.astype(out_ref.dtype)
-
-
-def place(slot_of, wide, up, before, owners):
-    strip, width = up.shape[1:]
-    earlier = [] if before is None else [before]
-    columns = width + sum(a.shape[2] for a in earlier)
+        out_ref[:, pl.ds(0, ref.shape[1])] = ref[...]
+    out_ref[:, pl.ds(out_ref.shape[1] - width, width)] = jnp.dot(
+        put_ref[...], total.reshape(-1, width), preferred_element_type=jnp.float32
+    ).astype(out_ref.dtype)
+
+
+def place(put, wide, got, *before):
+    width = got.shape[2]
+    columns = width + sum(a.shape[1] for a in before)
     return pl.pallas_call(
         place_kernel,
-        out_shape=jax.ShapeDtypeStruct((owners, strip, columns), up.dtype),
-        in_specs=[SMEM] + [VMEM] * (2 + len(earlier)),
+        out_shape=jax.ShapeDtypeStruct((put.shape[0], columns), got.dtype),
+        in_specs=[VMEM] * (3 + len(before)),
         out_specs=VMEM,
         compiler_params=pltpu.CompilerParams(vmem_limit_bytes=8 << 20),
         cost_estimate=pl.CostEstimate(flops=0, bytes_accessed=WAIT_BYTES, transcendentals=0),
         name="place",
-    )(slot_of, near(wide), near(up), *[near(a) for a in earlier])
+    )(*[near(a) for a in (put, wide, got) + before])
 
 
 def step_kernel(block_ref, left_ref, right_ref, out_ref, precond_ref):
     size = block_ref.shape[0]
-    tile = size // 4
+    tile = size
     block = block_ref[...]
     squares = jnp.zeros((tile, size), jnp.float32)
     inputs = jnp.zeros((tile, size), jnp.float32)
-    for i in range(4):
+    for i in range(1):
         rows = pl.ds(i * tile, tile)
         wide = block_ref[rows, :].astype(jnp.float32)
         inputs += wide * wide
@@ -151,7 +187,7 @@
     ratio = jnp.sqrt(jnp.sum(inputs, keepdims=True) * count + EPSILON) / jnp.sqrt(
         jnp.sum(squares, keepdims=True) * count + EPSILON
     )
-    for i in range(4):
+    for i in range(1):
         rows = pl.ds(i * tile, tile)
         out_ref[rows, :] = (precond_ref[rows, :] * ratio).astype(out_ref.dtype)
 
@@ -172,27 +208,45 @@
     )(near(block), near(left_root), near(right_root))
 
 
-def pick_kernel(slot_ref, rows_ref, out_ref):
-    for b in range(out_ref.shape[0]):
-        out_ref[b] = rows_ref[slot_ref[b]].astype(out_ref.dtype)
-
-
-def pick(slot_of, rows):
+def pick_kernel(take_ref, rows_ref, out_ref, wide_ref, sems):
+    chunks = sems.shape[0]
+    count, strip, width = wide_ref.shape[0] // chunks, *wide_ref.shape[1:]
+    copies = []
+    for chunk in range(chunks):
+        blocks = pl.ds(chunk * count, count)
+        picked = jnp.dot(
+            take_ref[pl.ds(chunk * count * strip, count * strip), :],
+            rows_ref[...],
+            preferred_element_type=jnp.float32,
+        )
+        wide_ref[blocks] = picked.reshape(count, strip, width)
+        copy = pltpu.make_async_copy(wide_ref.at[blocks], out_ref.at[blocks], sems.at[chunk])
+        copy.start()
+        copies.append(copy)
+    for copy in copies:
+        copy.wait()
+
+
+def pick(take, rows, strip):
+    width = rows.shape[1]
+    shape = (take.shape[0] // strip, strip, width)
     return pl.pallas_call(
         pick_kernel,
-        out_shape=jax.ShapeDtypeStruct(slot_of.shape + rows.shape[1:], jnp.float32),
-        in_specs=[SMEM, VMEM],
-        out_specs=VMEM,
+        out_shape=jax.ShapeDtypeStruct(shape, jnp.float32),
+        in_specs=[VMEM, VMEM],
+        out_specs=pl.BlockSpec(memory_space=pltpu.HBM),
+        scratch_shapes=[pltpu.VMEM(shape, jnp.float32), pltpu.SemaphoreType.DMA((3,))],
         compiler_params=pltpu.CompilerParams(vmem_limit_bytes=8 << 20),
         cost_estimate=pl.CostEstimate(flops=0, bytes_accessed=1_300_000, transcendentals=0),
         name="pick",
-    )(slot_of, near(rows))
+    )(near(take), near(rows))
 
 
 def local(grads, slot_of, left_stats, right_stats, left_roots, right_roots):
     replicas, owners = lax.axis_size("rep"), lax.axis_size("own")
-    downs, ups, own, last = chains(grads[0], replicas)
-    strip, width = own.shape[1:]
+    strip, width = grads.shape[2:]
+    chosen = selections(slot_of, owners, strip)
+    downs, ups, own, last, (put, take) = chains(grads[0], replicas, chosen)
     block_size = strip * owners
 
     near_down, near_up = downs[1], ups[0]
@@ -201,9 +255,8 @@
     wide_last, near_up = ordered(wide_last, near_up)
     wide_first = widen(own, near_up, 0)
     wide_first, far_down = ordered(wide_first, downs[0])
-    sends = place(slot_of, wide_first, far_down, None, owners)
-    sends, far_up = ordered(sends, ups[1])
-    sends = place(slot_of, wide_last, far_up, sends, owners)
+    first = place(put, wide_first, far_down)
+    sends = place(put, wide_last, ups[1], first).reshape(owners, strip, width)
     block = lax.all_to_all(sends, "own", 0, 0, tiled=True).reshape(block_size, width)
 
     grafted = graft(block, left_roots[0, 0], right_roots[0, 0]).reshape(owners, strip, width)
@@ -214,7 +267,7 @@
     left_next = DECAY * left_stats[0, 0] + (1.0 - DECAY) * gram_left
     right_next = DECAY * right_stats[0, 0] + (1.0 - DECAY) * gram_right
 
-    update = pick(slot_of, rows)
+    update = pick(take, rows.reshape(block_size, width), strip)
     return left_next[None, None], right_next[None, None], update
 
 

time: 82.6 us -> 77.9 us (0.943)
  starting transfers between devices: 30.7 us -> 27.3 us
  waiting for transfers between devices: 17.7 us -> 15.3 us
  blocking collectives: 22.7 us -> 21.3 us
  matrix products: 2.9 us -> 4.12 us
  Pallas kernels: 5.27 us -> 6.1 us
    ppermute x10, starting transfers between devices: 17.7 us -> 14.3 us  [chains(): array[part] = lax.ppermute(last, 'rep', pairs)]
    all_to_all x1, blocking collectives: 22.7 us -> 21.3 us  [local(): lax.all_to_all(sends, 'own', 0, 0, tiled=True).reshape(block_size, width)]
    ppermute x4, waiting for transfers between devices: 1.28 us -> 0.01 us  [the longest x2 0.01 us: chains(): lax.ppermute(two, 'rep', ahead)]
    dot_general x1, matrix products: 1.45 us -> 2.68 us  [local(): jnp.einsum('ki,kj->ij', block, block, preferred_element_type=jnp.float32)]
    all_to_all x1, waiting for transfers between devices: 8.66 us -> 7.46 us  [local(): rows = lax.all_to_all(grafted, 'own', 0, 0, tiled=True)]
    pallas_call x3 -> x5, Pallas kernels: 2.67 us -> 3.84 us  [the longest x2 2.09 us: slices(): pl.pallas_call(functools.partial(slice_kernel, picks=picks), out_shape=[j...]
  transfers between devices with their start and end apart: 15 -> 15, of which waited for: 9 -> 6; matrix products, arithmetic and copies ran while one was open for 4% -> 9% of each run, Pallas kernels for 1% -> 2%
where the time goes in v2:
time: 77.9 us; the launch traced here: 77.6 us
  starting transfers between devices  27.3 us (35%)
  blocking collectives  21.3 us (27%)
  waiting for transfers between devices  15.3 us (20%)
  Pallas kernels  6.1 us (8%)
  matrix products  4.12 us (5%)
  local copies, waits for them, and re-layouts  2.15 us (3%)
  between operations  1.06 us (1%)
    all_to_all x1, blocking collectives, local(): lax.all_to_all(sends, 'own', 0, 0, tiled=True).reshape(block_size, width)  21.3 us
    ppermute x10, starting transfers between devices, chains(): array[part] = lax.ppermute(last, 'rep', pairs)  14.3 us
    ppermute x10, waiting for transfers between devices, chains(): array[part] = lax.ppermute(last, 'rep', pairs)  7.79 us
    all_to_all x1, waiting for transfers between devices, local(): rows = lax.all_to_all(grafted, 'own', 0, 0, tiled=True)  7.46 us
    ppermute x2, starting transfers between devices, chains(): lax.ppermute(two, 'rep', ahead)  6.69 us
    all_to_all x1, starting transfers between devices, local(): rows = lax.all_to_all(grafted, 'own', 0, 0, tiled=True)  3.68 us
    dot_general x1, matrix products, local(): jnp.einsum('ki,kj->ij', block, block, preferred_element_type=jnp.float32)  2.68 us
    ppermute x2, starting transfers between devices, chains(): lax.ppermute(one, 'rep', back)  2.63 us
  transfers between devices with their start and end apart: 15, of which 6 were waited for; matrix products, arithmetic and copies ran while one was open for 9% of the time, Pallas kernels for 2%

profile of v2, /device:TPU:1, one launch (start us, length us, event | category | flops | bytes accessed | tf_op | source)
XLA Modules:
  0.0 77.6 jit_solution(17956508354784018456)
XLA Ops:
  0.6 1.1 %slices.2 = (bf16[24,16,256]{2,1,0:T(8,128)(2,1)S(1)}, bf16[24,16,256]{2,1,0:T(8,128)(2,1)S(1)}) custom-call(bf16[8,24,16,512]{3,2,1,0:T(8,128)(2,1)} %bitcast.47), custom_call_target="tpu_custom_call" | custom-call | bytes 1000000 | tf_op jit(solution)/shard_map/slices/pallas_call | solution.py:41
  1.7 2.5 %collective-permute-start = (bf16[24,16,256]{2,1,0:T(8,128)(2,1)S(1)}, bf16[24,16,256]{2,1,0:T(8,128)(2,1)S(1)}, u32[]{:S(2)}, u32[]{:S(2)}) collective-permute-start(bf16[24,16,256]{2,1,0:T(8,128)(2,1)S(1)} %get-tuple-element.29), channel_id=1, source_target_pairs={{0,32},{32,64},{64,96},{96,128},{128,160},{160,192},{192,224},{224... | collective-permute-start | bytes 589832 | tf_op jit(solution)/shard_map/ppermute | solution.py:92
  4.2 4.0 %collective-permute-start.1 = (bf16[24,16,256]{2,1,0:T(8,128)(2,1)S(1)}, bf16[24,16,256]{2,1,0:T(8,128)(2,1)S(1)}, u32[]{:S(2)}, u32[]{:S(2)}) collective-permute-start(bf16[24,16,256]{2,1,0:T(8,128)(2,1)S(1)} %get-tuple-element.33), channel_id=1, source_target_pairs={{0,224},{32,0},{64,32},{96,64},{128,96},{160,128},{192,160},{224,1... | collective-permute-start | bytes 589832 | tf_op jit(solution)/shard_map/ppermute | solution.py:92
  8.3 1.0 %slices.3 = (bf16[24,16,256]{2,1,0:T(8,128)(2,1)S(1)}, bf16[24,16,256]{2,1,0:T(8,128)(2,1)S(1)}) custom-call(bf16[8,24,16,512]{3,2,1,0:T(8,128)(2,1)} %bitcast.48), custom_call_target="tpu_custom_call" | custom-call | bytes 1000000 | tf_op jit(solution)/shard_map/slices/pallas_call | solution.py:41
  9.3 0.1 collective-permute-start.2
  9.4 2.7 %collective-permute-start.3 = (bf16[24,16,256]{2,1,0:T(8,128)(2,1)S(1)}, bf16[24,16,256]{2,1,0:T(8,128)(2,1)S(1)}, u32[]{:S(2)}, u32[]{:S(2)}) collective-permute-start(bf16[24,16,256]{2,1,0:T(8,128)(2,1)S(1)} %get-tuple-element.36), channel_id=1, source_target_pairs={{0,224},{32,0},{64,32},{96,64},{128,96},{160,128},{192,160},{224,1... | collective-permute-start | bytes 589832 | tf_op jit(solution)/shard_map/ppermute | solution.py:95
  12.1 0.1 broadcast_in_dim.6
  12.2 0.1 eq.74
  12.2 2.0 %dynamic-slice_bitcast_fusion = (bf16[24,16,512]{2,1,0:T(8,128)(2,1)S(1)}, bf16[24,16,512]{2,1,0:T(8,128)(2,1)S(1)}, bf16[24,16,512]{2,1,0:T(8,128)(2,1)S(1)}, b...) fusion(bf16[8,24,16,512]{3,2,1,0:T(8,128)(2,1)} %bitcast.49, ...), kind=kLoop, calls=%fused_computation.9 | loop fusion | bytes 5505052 | tf_op jit(solution)/shard_map/jit(dynamic_index_in_dim)/squeeze | solution.py:88
  14.2 0.0 collective-permute-done.got_ref
  14.3 0.1 collective-permute-start.4
  14.4 0.0 collective-permute-done.1.got_ref
  14.4 2.7 %collective-permute-start.5 = (bf16[24,16,256]{2,1,0:T(8,128)(2,1)S(1)}, bf16[24,16,256]{2,1,0:T(8,128)(2,1)S(1)}, u32[]{:S(2)}, u32[]{:S(2)}) collective-permute-start(bf16[24,16,256]{2,1,0:T(8,128)(2,1)S(1)} %add.205), channel_id=1, source_target_pairs={{0,224},{32,0},{64,32},{96,64},{128,96},{160,128},{192,160},{224,1... | collective-permute-start | bytes 589832 | tf_op jit(solution)/shard_map/ppermute | solution.py:112
  17.1 0.2 and_convert_fusion.take_ref
  17.3 0.0 collective-permute-done.2.got_ref
  17.4 0.1 collective-permute-start.6
  17.4 0.0 collective-permute-done.3.got_ref
  17.5 2.7 %collective-permute-start.7 = (bf16[24,16,256]{2,1,0:T(8,128)(2,1)S(1)}, bf16[24,16,256]{2,1,0:T(8,128)(2,1)S(1)}, u32[]{:S(2)}, u32[]{:S(2)}) collective-permute-start(bf16[24,16,256]{2,1,0:T(8,128)(2,1)S(1)} %add.207), channel_id=1, source_target_pairs={{0,224},{32,0},{64,32},{96,64},{128,96},{160,128},{192,160},{224,1... | collective-permute-start | bytes 589832 | tf_op jit(solution)/shard_map/ppermute | solution.py:112
  20.2 0.2 collective-permute-done.4.got_ref
  20.5 0.1 collective-permute-start.8
  20.5 0.0 collective-permute-done.5.got_ref
  20.6 2.7 %collective-permute-start.9 = (bf16[24,16,256]{2,1,0:T(8,128)(2,1)S(1)}, bf16[24,16,256]{2,1,0:T(8,128)(2,1)S(1)}, u32[]{:S(2)}, u32[]{:S(2)}) collective-permute-start(bf16[24,16,256]{2,1,0:T(8,128)(2,1)S(1)} %add.209), channel_id=1, source_target_pairs={{0,224},{32,0},{64,32},{96,64},{128,96},{160,128},{192,160},{224,1... | collective-permute-start | bytes 589832 | tf_op jit(solution)/shard_map/ppermute | solution.py:112
  23.3 0.2 and_convert_fusion.1.put_ref
  23.5 1.7 %collective-permute-done.6.got_ref = bf16[24,16,256]{2,1,0:T(8,128)(2,1)S(1)} collective-permute-done((bf16[24,16,256]{2,1,0:T(8,128)(2,1)S(1)}, bf16[24,16,256]{2,1,0:T(8,128)(2,1)S(1)}, u32[]{:S(2)}, u32[]{:S(2)}) %collective-permute-start.6) | collective-permute-done | bytes 196640 | tf_op jit(solution)/shard_map/ppermute | solution.py:112
  25.2 0.1 collective-permute-start.10
  25.3 0.0 collective-permute-done.7.got_ref
  25.4 2.8 %collective-permute-start.11 = (bf16[24,16,256]{2,1,0:T(8,128)(2,1)S(1)}, bf16[24,16,256]{2,1,0:T(8,128)(2,1)S(1)}, u32[]{:S(2)}, u32[]{:S(2)}) collective-permute-start(bf16[24,16,256]{2,1,0:T(8,128)(2,1)S(1)} %add.211), channel_id=1, source_target_pairs={{0,224},{32,0},{64,32},{96,64},{128,96},{160,128},{192,160},{224,1... | collective-permute-start | bytes 589832 | tf_op jit(solution)/shard_map/ppermute | solution.py:112
  28.1 1.0 %collective-permute-done.8.got_ref = bf16[24,16,256]{2,1,0:T(8,128)(2,1)S(1)} collective-permute-done((bf16[24,16,256]{2,1,0:T(8,128)(2,1)S(1)}, bf16[24,16,256]{2,1,0:T(8,128)(2,1)S(1)}, u32[]{:S(2)}, u32[]{:S(2)}) %collective-permute-start.8) | collective-permute-done | bytes 196640 | tf_op jit(solution)/shard_map/ppermute | solution.py:112
  29.1 0.1 collective-permute-start.13
  29.2 0.0 collective-permute-done.9.got_ref
  29.2 0.0 copy-start
  29.2 0.0 copy-start.1
  29.3 2.9 %collective-permute-start.12 = (bf16[24,16,256]{2,1,0:T(8,128)(2,1)S(1)}, bf16[24,16,256]{2,1,0:T(8,128)(2,1)S(1)}, u32[]{:S(2)}, u32[]{:S(2)}) collective-permute-start(bf16[24,16,256]{2,1,0:T(8,128)(2,1)S(1)} %add.213), channel_id=1, source_target_pairs={{0,224},{32,0},{64,32},{96,64},{128,96},{160,128},{192,160},{224,1... | collective-permute-start | bytes 589832 | tf_op jit(solution)/shard_map/ppermute | solution.py:112
  32.2 0.5 collective-permute-done.10.down_ref
  32.8 0.0 collective-permute-done.11.down_ref
  32.8 0.1 widen.3.wide_ref
  32.8 4.4 %collective-permute-done.13.got_ref = bf16[24,16,256]{2,1,0:T(8,128)(2,1)S(1)} collective-permute-done((bf16[24,16,256]{2,1,0:T(8,128)(2,1)S(1)}, bf16[24,16,256]{2,1,0:T(8,128)(2,1)S(1)}, u32[]{:S(2)}, u32[]{:S(2)}) %collective-permute-start.13) | collective-permute-done | bytes 196640 | tf_op jit(solution)/shard_map/ppermute | solution.py:112
  37.2 0.3 place.2.refs_0_
  37.5 0.0 copy-start.2
  37.5 0.0 collective-permute-done.12.got_ref
  37.5 0.3 place.3
  37.9 21.3 %all_to_all.10 = bf16[32,16,512]{2,1,0:T(8,128)(2,1)S(1)} all-to-all(bf16[32,16,512]{2,1,0:T(8,128)(2,1)S(1)} %bitcast.43), channel_id=1, replica_groups=mesh['rep'=8,'own'=32] {'own'}, dimensions={0} | all-to-all | bytes 1048576 | tf_op jit(solution)/shard_map/all_to_all | solution.py:260
  59.1 1.9 %graft.1 = bf16[512,512]{1,0:T(8,128)(2,1)} custom-call(bf16[512,512]{1,0:T(8,128)(2,1)S(1)} %bitcast.41, bf16[512,512]{1,0:T(8,128)(2,1)S(1)} %bitcast.45, bf16[512,512]{1,0:T(8,128)(2,1)S(1)} %bitcast.46), custom_call_target="tpu_custom_call" | custom-call | flops 536870912 | bytes 2097152 | tf_op jit(solution)/shard_map/graft/pallas_call | solution.py:197
  61.0 3.7 %all-to-all-start.1 = ((bf16[32,16,512]{2,1,0:T(8,128)(2,1)}), bf16[32,16,512]{2,1,0:T(8,128)(2,1)S(1)}, u32[]{:S(2)}, u32[]{:S(2)}) async-start(bf16[32,16,512]{2,1,0:T(8,128)(2,1)} %bitcast.17), calls=%async_computation.1 | async-start | bytes 1048576 | tf_op jit(solution)/shard_map/all_to_all | solution.py:263
  64.7 1.4 %fusion.2 = f32[1,1,512,512]{3,2,1,0:T(8,128)} fusion(bf16[512,512]{1,0:T(8,128)(2,1)S(1)} %bitcast.42, f32[1,1,512,512]{3,2,1,0:T(8,128)S(1)} %copy-done.2), kind=kOutput, calls=%fused_computation.4 | convolution fusion | flops 269221888 | bytes 2621440 | tf_op jit(solution)/shard_map/ik,jk->ij/dot_general | solution.py:265
  66.2 2.7 %fusion.4 = f32[1,1,512,512]{3,2,1,0:T(8,128)} fusion(bf16[32,16,512]{2,1,0:T(8,128)(2,1)S(1)} %all_to_all.10, f32[1,1,512,512]{3,2,1,0:T(8,128)} %param.9), kind=kOutput, calls=%fused_computation.6 | convolution fusion | flops 269221888 | bytes 2621440 | tf_op jit(solution)/shard_map/ki,kj->ij/dot_general | solution.py:266
  68.9 7.5 %all-to-all-done.1 = bf16[32,16,512]{2,1,0:T(8,128)(2,1)S(1)} async-done(((bf16[32,16,512]{2,1,0:T(8,128)(2,1)}), bf16[32,16,512]{2,1,0:T(8,128)(2,1)S(1)}, u32[]{:S(2)}, u32[]{:S(2)}) %all-to-all-start.1) | async-done | bytes 524320 | tf_op jit(solution)/shard_map/all_to_all | solution.py:263
  76.3 1.1 %pick.1 = f32[24,16,512]{2,1,0:T(8,128)} custom-call(bf16[384,512]{1,0:T(8,128)(2,1)S(1)} %and_convert_fusion.take_ref, bf16[512,512]{1,0:T(8,128)(2,1)S(1)} %bitcast.44), custom_call_target="tpu_custom_call" | custom-call | bytes 1300000 | tf_op jit(solution)/shard_map/pick/pallas_call | solution.py:233
  (18 shorter events, 0.3 us)
Async XLA Ops:
  0.6 11.5 %copy-start.3 = (s32[24]{0:T(128)S(1)}, s32[24]{0:T(128)}, u32[]{:S(2)}) copy-start(s32[24]{0:T(128)} %param.7) | copy-start | bytes 292
  1.7 12.5 %collective-permute-start = (bf16[24,16,256]{2,1,0:T(8,128)(2,1)S(1)}, bf16[24,16,256]{2,1,0:T(8,128)(2,1)S(1)}, u32[]{:S(2)}, u32[]{:S(2)}) collective-permute-start(bf16[24,16,256]{2,1,0:T(8,128)(2,1)S(1)} %get-tuple-element.29), channel_id=1, source_target_pairs={{0,32},{32,64},{64,96},{96,128},{128,160},{160,192},{192,224},{224... | collective-permute-start | bytes 589832 | tf_op jit(solution)/shard_map/ppermute | solution.py:92
  4.2 10.1 %collective-permute-start.1 = (bf16[24,16,256]{2,1,0:T(8,128)(2,1)S(1)}, bf16[24,16,256]{2,1,0:T(8,128)(2,1)S(1)}, u32[]{:S(2)}, u32[]{:S(2)}) collective-permute-start(bf16[24,16,256]{2,1,0:T(8,128)(2,1)S(1)} %get-tuple-element.33), channel_id=1, source_target_pairs={{0,224},{32,0},{64,32},{96,64},{128,96},{160,128},{192,160},{224,1... | collective-permute-start | bytes 589832 | tf_op jit(solution)/shard_map/ppermute | solution.py:92
  9.3 8.0 %collective-permute-start.2 = (bf16[24,16,256]{2,1,0:T(8,128)(2,1)S(1)}, bf16[24,16,256]{2,1,0:T(8,128)(2,1)S(1)}, u32[]{:S(2)}, u32[]{:S(2)}) collective-permute-start(bf16[24,16,256]{2,1,0:T(8,128)(2,1)S(1)} %get-tuple-element.31), channel_id=1, source_target_pairs={{0,32},{32,64},{64,96},{96,128},{128,160},{160,192},{192,224},{224... | collective-permute-start | bytes 589832 | tf_op jit(solution)/shard_map/ppermute | solution.py:95
  9.4 8.0 %collective-permute-start.3 = (bf16[24,16,256]{2,1,0:T(8,128)(2,1)S(1)}, bf16[24,16,256]{2,1,0:T(8,128)(2,1)S(1)}, u32[]{:S(2)}, u32[]{:S(2)}) collective-permute-start(bf16[24,16,256]{2,1,0:T(8,128)(2,1)S(1)} %get-tuple-element.36), channel_id=1, source_target_pairs={{0,224},{32,0},{64,32},{96,64},{128,96},{160,128},{192,160},{224,1... | collective-permute-start | bytes 589832 | tf_op jit(solution)/shard_map/ppermute | solution.py:95
  14.3 6.2 %collective-permute-start.4 = (bf16[24,16,256]{2,1,0:T(8,128)(2,1)S(1)}, bf16[24,16,256]{2,1,0:T(8,128)(2,1)S(1)}, u32[]{:S(2)}, u32[]{:S(2)}) collective-permute-start(bf16[24,16,256]{2,1,0:T(8,128)(2,1)S(1)} %add.204), channel_id=1, source_target_pairs={{0,32},{32,64},{64,96},{96,128},{128,160},{160,192},{192,224},{224... | collective-permute-start | bytes 589832 | tf_op jit(solution)/shard_map/ppermute | solution.py:112
  14.4 6.2 %collective-permute-start.5 = (bf16[24,16,256]{2,1,0:T(8,128)(2,1)S(1)}, bf16[24,16,256]{2,1,0:T(8,128)(2,1)S(1)}, u32[]{:S(2)}, u32[]{:S(2)}) collective-permute-start(bf16[24,16,256]{2,1,0:T(8,128)(2,1)S(1)} %add.205), channel_id=1, source_target_pairs={{0,224},{32,0},{64,32},{96,64},{128,96},{160,128},{192,160},{224,1... | collective-permute-start | bytes 589832 | tf_op jit(solution)/shard_map/ppermute | solution.py:112
  17.4 7.8 %collective-permute-start.6 = (bf16[24,16,256]{2,1,0:T(8,128)(2,1)S(1)}, bf16[24,16,256]{2,1,0:T(8,128)(2,1)S(1)}, u32[]{:S(2)}, u32[]{:S(2)}) collective-permute-start(bf16[24,16,256]{2,1,0:T(8,128)(2,1)S(1)} %add.206), channel_id=1, source_target_pairs={{0,32},{32,64},{64,96},{96,128},{128,160},{160,192},{192,224},{224... | collective-permute-start | bytes 589832 | tf_op jit(solution)/shard_map/ppermute | solution.py:112
  17.5 7.8 %collective-permute-start.7 = (bf16[24,16,256]{2,1,0:T(8,128)(2,1)S(1)}, bf16[24,16,256]{2,1,0:T(8,128)(2,1)S(1)}, u32[]{:S(2)}, u32[]{:S(2)}) collective-permute-start(bf16[24,16,256]{2,1,0:T(8,128)(2,1)S(1)} %add.207), channel_id=1, source_target_pairs={{0,224},{32,0},{64,32},{96,64},{128,96},{160,128},{192,160},{224,1... | collective-permute-start | bytes 589832 | tf_op jit(solution)/shard_map/ppermute | solution.py:112
  20.5 8.6 %collective-permute-start.8 = (bf16[24,16,256]{2,1,0:T(8,128)(2,1)S(1)}, bf16[24,16,256]{2,1,0:T(8,128)(2,1)S(1)}, u32[]{:S(2)}, u32[]{:S(2)}) collective-permute-start(bf16[24,16,256]{2,1,0:T(8,128)(2,1)S(1)} %add.208), channel_id=1, source_target_pairs={{0,32},{32,64},{64,96},{96,128},{128,160},{160,192},{192,224},{224... | collective-permute-start | bytes 589832 | tf_op jit(solution)/shard_map/ppermute | solution.py:112
  20.6 8.6 %collective-permute-start.9 = (bf16[24,16,256]{2,1,0:T(8,128)(2,1)S(1)}, bf16[24,16,256]{2,1,0:T(8,128)(2,1)S(1)}, u32[]{:S(2)}, u32[]{:S(2)}) collective-permute-start(bf16[24,16,256]{2,1,0:T(8,128)(2,1)S(1)} %add.209), channel_id=1, source_target_pairs={{0,224},{32,0},{64,32},{96,64},{128,96},{160,128},{192,160},{224,1... | collective-permute-start | bytes 589832 | tf_op jit(solution)/shard_map/ppermute | solution.py:112
  25.2 7.5 %collective-permute-start.10 = (bf16[24,16,256]{2,1,0:T(8,128)(2,1)S(1)}, bf16[24,16,256]{2,1,0:T(8,128)(2,1)S(1)}, u32[]{:S(2)}, u32[]{:S(2)}) collective-permute-start(bf16[24,16,256]{2,1,0:T(8,128)(2,1)S(1)} %add.210), channel_id=1, source_target_pairs={{0,32},{32,64},{64,96},{96,128},{128,160},{160,192},{192,224},{224... | collective-permute-start | bytes 589832 | tf_op jit(solution)/shard_map/ppermute | solution.py:112
  25.4 7.4 %collective-permute-start.11 = (bf16[24,16,256]{2,1,0:T(8,128)(2,1)S(1)}, bf16[24,16,256]{2,1,0:T(8,128)(2,1)S(1)}, u32[]{:S(2)}, u32[]{:S(2)}) collective-permute-start(bf16[24,16,256]{2,1,0:T(8,128)(2,1)S(1)} %add.211), channel_id=1, source_target_pairs={{0,224},{32,0},{64,32},{96,64},{128,96},{160,128},{192,160},{224,1... | collective-permute-start | bytes 589832 | tf_op jit(solution)/shard_map/ppermute | solution.py:112
  29.1 8.1 %collective-permute-start.13 = (bf16[24,16,256]{2,1,0:T(8,128)(2,1)S(1)}, bf16[24,16,256]{2,1,0:T(8,128)(2,1)S(1)}, u32[]{:S(2)}, u32[]{:S(2)}) collective-permute-start(bf16[24,16,256]{2,1,0:T(8,128)(2,1)S(1)} %add.212), channel_id=1, source_target_pairs={{0,32},{32,64},{64,96},{96,128},{128,160},{160,192},{192,224},{224... | collective-permute-start | bytes 589832 | tf_op jit(solution)/shard_map/ppermute | solution.py:112
  29.2 29.9 %copy-start = (bf16[1,1,512,512]{3,2,1,0:T(8,128)(2,1)S(1)}, bf16[1,1,512,512]{3,2,1,0:T(8,128)(2,1)}, u32[]{:S(2)}) copy-start(bf16[1,1,512,512]{3,2,1,0:T(8,128)(2,1)} %param.10) | copy-start | bytes 1572868
  29.2 29.9 %copy-start.1 = (bf16[1,1,512,512]{3,2,1,0:T(8,128)(2,1)S(1)}, bf16[1,1,512,512]{3,2,1,0:T(8,128)(2,1)}, u32[]{:S(2)}) copy-start(bf16[1,1,512,512]{3,2,1,0:T(8,128)(2,1)} %param.11) | copy-start | bytes 1572868
  29.3 8.3 %collective-permute-start.12 = (bf16[24,16,256]{2,1,0:T(8,128)(2,1)S(1)}, bf16[24,16,256]{2,1,0:T(8,128)(2,1)S(1)}, u32[]{:S(2)}, u32[]{:S(2)}) collective-permute-start(bf16[24,16,256]{2,1,0:T(8,128)(2,1)S(1)} %add.213), channel_id=1, source_target_pairs={{0,224},{32,0},{64,32},{96,64},{128,96},{160,128},{192,160},{224,1... | collective-permute-start | bytes 589832 | tf_op jit(solution)/shard_map/ppermute | solution.py:112
  37.5 27.2 %copy-start.2 = (f32[1,1,512,512]{3,2,1,0:T(8,128)S(1)}, f32[1,1,512,512]{3,2,1,0:T(8,128)}, u32[]{:S(2)}) copy-start(f32[1,1,512,512]{3,2,1,0:T(8,128)} %param.8) | copy-start | bytes 3145732
  61.0 15.3 %all-to-all-start.1 = ((bf16[32,16,512]{2,1,0:T(8,128)(2,1)}), bf16[32,16,512]{2,1,0:T(8,128)(2,1)S(1)}, u32[]{:S(2)}, u32[]{:S(2)}) async-start(bf16[32,16,512]{2,1,0:T(8,128)(2,1)} %bitcast.17), calls=%async_computation.1 | async-start | bytes 1048576 | tf_op jit(solution)/shard_map/all_to_all | solution.py:263

commit v3 on v2

--- a/solution.py
+++ b/solution.py
@@ -22,13 +22,18 @@
     return lax.optimization_barrier((first, second))
 
 
+def half_of(width, parity):
+    part = lax.rem(lax.axis_index("rep") + parity, 2)
+    return pl.ds(pl.multiple_of(part * width, width), width)
+
+
 def slice_kernel(groups_ref, one_ref, two_ref, sems, *, picks):
-    me = lax.axis_index("rep")
-    width = one_ref.shape[2]
+    me, replicas = lax.axis_index("rep"), groups_ref.shape[0]
+    toward = 1 - 2 * lax.rem(me, 2)
     copies = []
-    for at, (out_ref, (ahead, part)) in enumerate(zip((one_ref, two_ref), picks)):
-        group = lax.rem(me + ahead, groups_ref.shape[0])
-        source = groups_ref.at[group, :, :, pl.ds(part * width, width)]
+    for at, (out_ref, (ahead, parity)) in enumerate(zip((one_ref, two_ref), picks)):
+        group = lax.rem(me + toward * ahead + replicas, replicas)
+        source = groups_ref.at[group, :, :, half_of(out_ref.shape[2], parity)]
         copies.append(pltpu.make_async_copy(source, out_ref, sems.at[at]))
     for copy in copies:
         copy.start()
@@ -51,8 +56,7 @@
 
 
 def add_kernel(got_ref, own_ref, out_ref, *, first, part):
-    width = out_ref.shape[2]
-    columns = pl.ds(part * width, width)
+    columns = half_of(out_ref.shape[2], part)
     blocks, got = out_ref.shape[0], got_ref.shape[0]
     if first > 0:
         out_ref[pl.ds(0, first)] = own_ref[pl.ds(0, first), :, columns]
@@ -79,43 +83,41 @@
 
 def chains(grads, replicas, chosen):
     me = lax.axis_index("rep")
+    toward = 1 - 2 * (me % 2)
     reach = replicas // 2
     groups = grads.reshape((replicas, -1) + grads.shape[1:])
-    ahead = [(i, (i - 1) % replicas) for i in range(replicas)]
-    back = [(i, (i + 1) % replicas) for i in range(replicas)]
-
-    def mine(group):
-        return lax.dynamic_index_in_dim(groups, (group + replicas) % replicas, 0, False)
-
-    down, up = [None, None], [None, None]
-    one, two = slices(groups, ((reach, 0), (reach, 1)))
-    down[0], up[1] = lax.ppermute(one, "rep", back), lax.ppermute(two, "rep", ahead)
+    partner = [(i, i + 1 if i % 2 == 0 else i - 1) for i in range(replicas)]
+    other = [(i, (i - 1 if i % 2 == 0 else i + 1) % replicas) for i in range(replicas)]
+
+    def mine(ahead):
+        return lax.dynamic_index_in_dim(groups, (me + toward * ahead + replicas) % replicas, 0, False)
+
+    one, two = slices(groups, ((reach, 1), (reach, 0)))
+    far = [lax.ppermute(one, "rep", partner), lax.ppermute(two, "rep", other)]
     one, groups = ordered(one, groups)
-    one, two = slices(groups, ((reach - 1, 1), (reach + 1, 0)))
-    down[1], up[0] = lax.ppermute(one, "rep", back), lax.ppermute(two, "rep", ahead)
+    one, two = slices(groups, ((reach - 1, 0), (1 - reach, 1)))
+    near_by = [lax.ppermute(one, "rep", partner), lax.ppermute(two, "rep", other)]
     one, groups = ordered(one, groups)
     last = None
     for step in range(reach - 1, 0, -1):
-        for at, one, two in ((step, 0, 1), (step - 1, 1, 0)):
+        for array, at, flip in ((far, step, 0), (near_by, step - 1, 1)):
             if at == 0:
                 continue
-            for array, part, group, pairs in (
-                (down, one, me + at, back),
-                (up, two, me - at, ahead),
-            ):
-                got = array[part]
+            passed = [None, None]
+            for side, ahead, pairs in ((0, -at, other), (1, at, partner)):
+                got = array[side]
                 if last is not None:
                     last, got = ordered(last, got)
                 if step == reach - 2 and not at == step:
                     chosen, got = ordered(chosen, got)
-                last = add(got, mine(group), 0, part)
-                array[part] = lax.ppermute(last, "rep", pairs)
-    return down, up, mine(me), last, chosen
+                last = add(got, mine(ahead), 0, (side + flip) % 2)
+                passed[1 - side] = lax.ppermute(last, "rep", pairs)
+            array[:] = passed
+    return far, near_by, mine(0), last, chosen
 
 
 def widen_kernel(own_ref, down_ref, out_ref, *, part):
-    width = out_ref.shape[2]
-    columns = pl.ds(part * width, width)
+    columns = half_of(out_ref.shape[2], part)
     out_ref[...] = down_ref[...].astype(jnp.float32) + own_ref[:, :, columns].astype(jnp.float32)
 
 
@@ -142,13 +144,18 @@
     return put.astype(jnp.bfloat16), take.astype(jnp.bfloat16)
 
 
-def place_kernel(put_ref, wide_ref, got_ref, *refs):
-    before, out_ref = refs[:-1], refs[-1]
+def put_kernel(put_ref, wide_ref, got_ref, out_ref):
+    total = (wide_ref[...] + got_ref[...].astype(jnp.float32)).astype(out_ref.dtype)
+    out_ref[...] = jnp.dot(
+        put_ref[...], total.reshape(-1, total.shape[2]), preferred_element_type=jnp.float32
+    ).astype(out_ref.dtype)
+
+
+def place_kernel(put_ref, wide_ref, got_ref, before_ref, out_ref):
     width = got_ref.shape[2]
     total = (wide_ref[...] + got_ref[...].astype(jnp.float32)).astype(out_ref.dtype)
-    for ref in before:
-        out_ref[:, pl.ds(0, ref.shape[1])] = ref[...]
-    out_ref[:, pl.ds(out_ref.shape[1] - width, width)] = jnp.dot(
+    out_ref[:, half_of(width, 1)] = before_ref[...]
+    out_ref[:, half_of(width, 0)] = jnp.dot(
         put_ref[...], total.reshape(-1, width), preferred_element_type=jnp.float32
     ).astype(out_ref.dtype)
 
@@ -157,7 +164,7 @@
     width = got.shape[2]
     columns = width + sum(a.shape[1] for a in before)
     return pl.pallas_call(
-        place_kernel,
+        place_kernel if before else put_kernel,
         out_shape=jax.ShapeDtypeStruct((put.shape[0], columns), got.dtype),
         in_specs=[VMEM] * (3 + len(before)),
         out_specs=VMEM,
@@ -246,17 +253,16 @@
     replicas, owners = lax.axis_size("rep"), lax.axis_size("own")
     strip, width = grads.shape[2:]
     chosen = selections(slot_of, owners, strip)
-    downs, ups, own, last, (put, take) = chains(grads[0], replicas, chosen)
+    far, near_by, own, last, (put, take) = chains(grads[0], replicas, chosen)
     block_size = strip * owners
 
-    near_down, near_up = downs[1], ups[0]
-    last, near_down = ordered(last, near_down)
-    wide_last = widen(own, near_down, 1)
-    wide_last, near_up = ordered(wide_last, near_up)
-    wide_first = widen(own, near_up, 0)
-    wide_first, far_down = ordered(wide_first, downs[0])
-    first = place(put, wide_first, far_down)
-    sends = place(put, wide_last, ups[1], first).reshape(owners, strip, width)
+    last, near_two = ordered(last, near_by[1])
+    wide_first = widen(own, near_two, 0)
+    wide_first, near_one = ordered(wide_first, near_by[0])
+    wide_last = widen(own, near_one, 1)
+    wide_last, far_two = ordered(wide_last, far[1])
+    first = place(put, wide_last, far_two)
+    sends = place(put, wide_first, far[0], first).reshape(owners, strip, width)
     block = lax.all_to_all(sends, "own", 0, 0, tiled=True).reshape(block_size, width)
 
     grafted = graft(block, left_roots[0, 0], right_roots[0, 0]).reshape(owners, strip, width)

time: 77.9 us -> 78.7 us (1.010)
  waiting for transfers between devices: 15.3 us -> 21 us
  starting transfers between devices: 27.3 us -> 21.7 us
    ppermute x14, waiting for transfers between devices: 7.8 us -> 13.6 us  [the longest x10 13.6 us: chains(): passed[1 - side] = lax.ppermute(last, 'rep', pairs)]
    ppermute x14, starting transfers between devices: 23.6 us -> 18 us  [the longest x10 9.26 us: chains(): passed[1 - side] = lax.ppermute(last, 'rep', pairs)]
  transfers between devices with their start and end apart: 15 -> 15, of which waited for: 6 -> 6; matrix products, arithmetic and copies ran while one was open for 9% -> 8% of each run, Pallas kernels for 2% -> 2%
where the time goes in v3:
time: 78.7 us; the launch traced here: 78.4 us
  blocking collectives  22 us (28%)
  starting transfers between devices  21.7 us (28%)
  waiting for transfers between devices  21 us (27%)
  Pallas kernels  6.14 us (8%)
  matrix products  4.12 us (5%)
  local copies, waits for them, and re-layouts  2.15 us (3%)
  between operations  0.89 us (1%)
    all_to_all x1, blocking collectives, local(): lax.all_to_all(sends, 'own', 0, 0, tiled=True).reshape(block_size, width)  22 us
    ppermute x10, waiting for transfers between devices, chains(): passed[1 - side] = lax.ppermute(last, 'rep', pairs)  13.6 us
    ppermute x10, starting transfers between devices, chains(): passed[1 - side] = lax.ppermute(last, 'rep', pairs)  9.26 us
    all_to_all x1, waiting for transfers between devices, local(): rows = lax.all_to_all(grafted, 'own', 0, 0, tiled=True)  7.42 us
    ppermute x2, starting transfers between devices, chains(): far = [lax.ppermute(one, 'rep', partner), lax.ppermute(two, 'rep', other)]  7.22 us
    all_to_all x1, starting transfers between devices, local(): rows = lax.all_to_all(grafted, 'own', 0, 0, tiled=True)  3.68 us
    dot_general x1, matrix products, local(): jnp.einsum('ki,kj->ij', block, block, preferred_element_type=jnp.float32)  2.67 us
    pallas_call x2, Pallas kernels, slices(): pl.pallas_call(functools.partial(slice_kernel, picks=picks), out_shape=[j...  2.1 us
  transfers between devices with their start and end apart: 15, of which 6 were waited for; matrix products, arithmetic and copies ran while one was open for 8% of the time, Pallas kernels for 2%

profile of v3, /device:TPU:1, one launch (start us, length us, event | category | flops | bytes accessed | tf_op | source)
XLA Modules:
  0.0 78.4 jit_solution(13849069036337736128)
XLA Ops:
  0.6 1.1 %slices.2 = (bf16[24,16,256]{2,1,0:T(8,128)(2,1)S(1)}, bf16[24,16,256]{2,1,0:T(8,128)(2,1)S(1)}) custom-call(bf16[8,24,16,512]{3,2,1,0:T(8,128)(2,1)} %bitcast.47), custom_call_target="tpu_custom_call" | custom-call | bytes 1000000 | tf_op jit(solution)/shard_map/slices/pallas_call | solution.py:46
  1.7 2.6 %collective-permute-start = (bf16[24,16,256]{2,1,0:T(8,128)(2,1)S(1)}, bf16[24,16,256]{2,1,0:T(8,128)(2,1)S(1)}, u32[]{:S(2)}, u32[]{:S(2)}) collective-permute-start(bf16[24,16,256]{2,1,0:T(8,128)(2,1)S(1)} %get-tuple-element.29), channel_id=1, source_target_pairs={{0,32},{32,0},{64,96},{96,64},{128,160},{160,128},{192,224},{224,1... | collective-permute-start | bytes 589832 | tf_op jit(solution)/shard_map/ppermute | solution.py:96
  4.3 4.7 %collective-permute-start.1 = (bf16[24,16,256]{2,1,0:T(8,128)(2,1)S(1)}, bf16[24,16,256]{2,1,0:T(8,128)(2,1)S(1)}, u32[]{:S(2)}, u32[]{:S(2)}) collective-permute-start(bf16[24,16,256]{2,1,0:T(8,128)(2,1)S(1)} %get-tuple-element.33), channel_id=1, source_target_pairs={{0,224},{32,64},{64,32},{96,128},{128,96},{160,192},{192,160},{224... | collective-permute-start | bytes 589832 | tf_op jit(solution)/shard_map/ppermute | solution.py:96
  8.9 1.0 %slices.3 = (bf16[24,16,256]{2,1,0:T(8,128)(2,1)S(1)}, bf16[24,16,256]{2,1,0:T(8,128)(2,1)S(1)}) custom-call(bf16[8,24,16,512]{3,2,1,0:T(8,128)(2,1)} %bitcast.48), custom_call_target="tpu_custom_call" | custom-call | bytes 1000000 | tf_op jit(solution)/shard_map/slices/pallas_call | solution.py:46
  10.0 0.1 collective-permute-start.2
  10.1 1.4 %collective-permute-start.3 = (bf16[24,16,256]{2,1,0:T(8,128)(2,1)S(1)}, bf16[24,16,256]{2,1,0:T(8,128)(2,1)S(1)}, u32[]{:S(2)}, u32[]{:S(2)}) collective-permute-start(bf16[24,16,256]{2,1,0:T(8,128)(2,1)S(1)} %get-tuple-element.36), channel_id=1, source_target_pairs={{0,224},{32,64},{64,32},{96,128},{128,96},{160,192},{192,160},{224... | collective-permute-start | bytes 589832 | tf_op jit(solution)/shard_map/ppermute | solution.py:99
  11.5 0.1 broadcast_in_dim.6
  11.6 0.1 eq.75
  11.7 2.0 %dynamic-slice_bitcast_fusion = (bf16[24,16,512]{2,1,0:T(8,128)(2,1)S(1)}, bf16[24,16,512]{2,1,0:T(8,128)(2,1)S(1)}, bf16[24,16,512]{2,1,0:T(8,128)(2,1)S(1)}, b...) fusion(bf16[8,24,16,512]{3,2,1,0:T(8,128)(2,1)} %bitcast.49, ...), kind=kLoop, calls=%fused_computation.9 | loop fusion | bytes 5505052 | tf_op jit(solution)/shard_map/jit(dynamic_index_in_dim)/squeeze | solution.py:93
  13.7 0.0 collective-permute-done.got_ref
  13.7 1.4 %collective-permute-start.5 = (bf16[24,16,256]{2,1,0:T(8,128)(2,1)S(1)}, bf16[24,16,256]{2,1,0:T(8,128)(2,1)S(1)}, u32[]{:S(2)}, u32[]{:S(2)}) collective-permute-start(bf16[24,16,256]{2,1,0:T(8,128)(2,1)S(1)} %add.216), channel_id=1, source_target_pairs={{0,224},{32,64},{64,32},{96,128},{128,96},{160,192},{192,160},{224... | collective-permute-start | bytes 589832 | tf_op jit(solution)/shard_map/ppermute | solution.py:114
  15.1 0.0 collective-permute-done.1.got_ref
  15.2 0.2 collective-permute-start.4
  15.4 0.2 and_convert_fusion.take_ref
  15.6 0.0 collective-permute-done.2.got_ref
  15.6 2.6 %collective-permute-start.7 = (bf16[24,16,256]{2,1,0:T(8,128)(2,1)S(1)}, bf16[24,16,256]{2,1,0:T(8,128)(2,1)S(1)}, u32[]{:S(2)}, u32[]{:S(2)}) collective-permute-start(bf16[24,16,256]{2,1,0:T(8,128)(2,1)S(1)} %add.218), channel_id=1, source_target_pairs={{0,224},{32,64},{64,32},{96,128},{128,96},{160,192},{192,160},{224... | collective-permute-start | bytes 589832 | tf_op jit(solution)/shard_map/ppermute | solution.py:114
  18.3 0.0 collective-permute-done.3.got_ref
  18.3 0.1 collective-permute-start.6
  18.4 1.6 %collective-permute-done.4.got_ref = bf16[24,16,256]{2,1,0:T(8,128)(2,1)S(1)} collective-permute-done((bf16[24,16,256]{2,1,0:T(8,128)(2,1)S(1)}, bf16[24,16,256]{2,1,0:T(8,128)(2,1)S(1)}, u32[]{:S(2)}, u32[]{:S(2)}) %collective-permute-start.4) | collective-permute-done | bytes 196640 | tf_op jit(solution)/shard_map/ppermute | solution.py:114
  20.1 1.5 %collective-permute-start.9 = (bf16[24,16,256]{2,1,0:T(8,128)(2,1)S(1)}, bf16[24,16,256]{2,1,0:T(8,128)(2,1)S(1)}, u32[]{:S(2)}, u32[]{:S(2)}) collective-permute-start(bf16[24,16,256]{2,1,0:T(8,128)(2,1)S(1)} %add.220), channel_id=1, source_target_pairs={{0,224},{32,64},{64,32},{96,128},{128,96},{160,192},{192,160},{224... | collective-permute-start | bytes 589832 | tf_op jit(solution)/shard_map/ppermute | solution.py:114
  21.6 0.0 collective-permute-done.5.got_ref
  21.6 0.1 collective-permute-start.8
  21.7 0.2 and_convert_fusion.1.put_ref
  21.9 3.4 %collective-permute-done.6.got_ref = bf16[24,16,256]{2,1,0:T(8,128)(2,1)S(1)} collective-permute-done((bf16[24,16,256]{2,1,0:T(8,128)(2,1)S(1)}, bf16[24,16,256]{2,1,0:T(8,128)(2,1)S(1)}, u32[]{:S(2)}, u32[]{:S(2)}) %collective-permute-start.6) | collective-permute-done | bytes 196640 | tf_op jit(solution)/shard_map/ppermute | solution.py:114
  25.3 1.2 %collective-permute-start.10 = (bf16[24,16,256]{2,1,0:T(8,128)(2,1)S(1)}, bf16[24,16,256]{2,1,0:T(8,128)(2,1)S(1)}, u32[]{:S(2)}, u32[]{:S(2)}) collective-permute-start(bf16[24,16,256]{2,1,0:T(8,128)(2,1)S(1)} %add.222), channel_id=1, source_target_pairs={{0,224},{32,64},{64,32},{96,128},{128,96},{160,192},{192,160},{224... | collective-permute-start | bytes 589832 | tf_op jit(solution)/shard_map/ppermute | solution.py:114
  26.5 0.0 collective-permute-done.7.got_ref
  26.6 0.1 collective-permute-start.11
  26.7 2.1 %collective-permute-done.8.got_ref = bf16[24,16,256]{2,1,0:T(8,128)(2,1)S(1)} collective-permute-done((bf16[24,16,256]{2,1,0:T(8,128)(2,1)S(1)}, bf16[24,16,256]{2,1,0:T(8,128)(2,1)S(1)}, u32[]{:S(2)}, u32[]{:S(2)}) %collective-permute-start.8) | collective-permute-done | bytes 196640 | tf_op jit(solution)/shard_map/ppermute | solution.py:114
  28.8 1.9 %collective-permute-start.13 = (bf16[24,16,256]{2,1,0:T(8,128)(2,1)S(1)}, bf16[24,16,256]{2,1,0:T(8,128)(2,1)S(1)}, u32[]{:S(2)}, u32[]{:S(2)}) collective-permute-start(bf16[24,16,256]{2,1,0:T(8,128)(2,1)S(1)} %add.224), channel_id=1, source_target_pairs={{0,224},{32,64},{64,32},{96,128},{128,96},{160,192},{192,160},{224... | collective-permute-start | bytes 589832 | tf_op jit(solution)/shard_map/ppermute | solution.py:114
  30.8 0.0 copy-start
  30.8 0.0 copy-start.1
  30.8 0.1 collective-permute-start.12
  30.9 2.8 %collective-permute-done.10.down_ref = bf16[24,16,256]{2,1,0:T(8,128)(2,1)S(1)} collective-permute-done((bf16[24,16,256]{2,1,0:T(8,128)(2,1)S(1)}, bf16[24,16,256]{2,1,0:T(8,128)(2,1)S(1)}, u32[]{:S(2)}, u32[]{:S(2)}) %collective-permute-start.10) | collective-permute-done | bytes 196640 | tf_op jit(solution)/shard_map/ppermute | solution.py:114
  33.7 0.1 widen.2.wide_ref
  33.8 0.0 collective-permute-done.11.down_ref
  33.8 0.1 widen.3.wide_ref
  33.8 3.6 %collective-permute-done.13.got_ref = bf16[24,16,256]{2,1,0:T(8,128)(2,1)S(1)} collective-permute-done((bf16[24,16,256]{2,1,0:T(8,128)(2,1)S(1)}, bf16[24,16,256]{2,1,0:T(8,128)(2,1)S(1)}, u32[]{:S(2)}, u32[]{:S(2)}) %collective-permute-start.13) | collective-permute-done | bytes 196640 | tf_op jit(solution)/shard_map/ppermute | solution.py:114
  37.5 0.3 place.2.before_ref
  37.8 0.0 copy-start.2
  37.8 0.0 collective-permute-done.12.got_ref
  37.8 0.3 place.3
  38.1 22.0 %all_to_all.10 = bf16[32,16,512]{2,1,0:T(8,128)(2,1)S(1)} all-to-all(bf16[32,16,512]{2,1,0:T(8,128)(2,1)S(1)} %bitcast.43), channel_id=1, replica_groups=mesh['rep'=8,'own'=32] {'own'}, dimensions={0} | all-to-all | bytes 1048576 | tf_op jit(solution)/shard_map/all_to_all | solution.py:266
  60.1 1.9 %graft.1 = bf16[512,512]{1,0:T(8,128)(2,1)} custom-call(bf16[512,512]{1,0:T(8,128)(2,1)S(1)} %bitcast.41, bf16[512,512]{1,0:T(8,128)(2,1)S(1)} %bitcast.45, bf16[512,512]{1,0:T(8,128)(2,1)S(1)} %bitcast.46), custom_call_target="tpu_custom_call" | custom-call | flops 536870912 | bytes 2097152 | tf_op jit(solution)/shard_map/graft/pallas_call | solution.py:204
  62.0 3.7 %all-to-all-start.1 = ((bf16[32,16,512]{2,1,0:T(8,128)(2,1)}), bf16[32,16,512]{2,1,0:T(8,128)(2,1)S(1)}, u32[]{:S(2)}, u32[]{:S(2)}) async-start(bf16[32,16,512]{2,1,0:T(8,128)(2,1)} %bitcast.17), calls=%async_computation.1 | async-start | bytes 1048576 | tf_op jit(solution)/shard_map/all_to_all | solution.py:269
  65.7 1.4 %fusion.2 = f32[1,1,512,512]{3,2,1,0:T(8,128)} fusion(bf16[512,512]{1,0:T(8,128)(2,1)S(1)} %bitcast.42, f32[1,1,512,512]{3,2,1,0:T(8,128)S(1)} %copy-done.2), kind=kOutput, calls=%fused_computation.4 | convolution fusion | flops 269221888 | bytes 2621440 | tf_op jit(solution)/shard_map/ik,jk->ij/dot_general | solution.py:271
  67.2 2.7 %fusion.4 = f32[1,1,512,512]{3,2,1,0:T(8,128)} fusion(bf16[32,16,512]{2,1,0:T(8,128)(2,1)S(1)} %all_to_all.10, f32[1,1,512,512]{3,2,1,0:T(8,128)} %param.9), kind=kOutput, calls=%fused_computation.6 | convolution fusion | flops 269221888 | bytes 2621440 | tf_op jit(solution)/shard_map/ki,kj->ij/dot_general | solution.py:272
  69.8 7.4 %all-to-all-done.1 = bf16[32,16,512]{2,1,0:T(8,128)(2,1)S(1)} async-done(((bf16[32,16,512]{2,1,0:T(8,128)(2,1)}), bf16[32,16,512]{2,1,0:T(8,128)(2,1)S(1)}, u32[]{:S(2)}, u32[]{:S(2)}) %all-to-all-start.1) | async-done | bytes 524320 | tf_op jit(solution)/shard_map/all_to_all | solution.py:269
  77.3 1.1 %pick.1 = f32[24,16,512]{2,1,0:T(8,128)} custom-call(bf16[384,512]{1,0:T(8,128)(2,1)S(1)} %and_convert_fusion.take_ref, bf16[512,512]{1,0:T(8,128)(2,1)S(1)} %bitcast.44), custom_call_target="tpu_custom_call" | custom-call | bytes 1300000 | tf_op jit(solution)/shard_map/pick/pallas_call | solution.py:240
  (18 shorter events, 0.3 us)
Async XLA Ops:
  0.6 10.9 %copy-start.3 = (s32[24]{0:T(128)S(1)}, s32[24]{0:T(128)}, u32[]{:S(2)}) copy-start(s32[24]{0:T(128)} %param.7) | copy-start | bytes 292
  1.7 12.0 %collective-permute-start = (bf16[24,16,256]{2,1,0:T(8,128)(2,1)S(1)}, bf16[24,16,256]{2,1,0:T(8,128)(2,1)S(1)}, u32[]{:S(2)}, u32[]{:S(2)}) collective-permute-start(bf16[24,16,256]{2,1,0:T(8,128)(2,1)S(1)} %get-tuple-element.29), channel_id=1, source_target_pairs={{0,32},{32,0},{64,96},{96,64},{128,160},{160,128},{192,224},{224,1... | collective-permute-start | bytes 589832 | tf_op jit(solution)/shard_map/ppermute | solution.py:96
  4.3 10.9 %collective-permute-start.1 = (bf16[24,16,256]{2,1,0:T(8,128)(2,1)S(1)}, bf16[24,16,256]{2,1,0:T(8,128)(2,1)S(1)}, u32[]{:S(2)}, u32[]{:S(2)}) collective-permute-start(bf16[24,16,256]{2,1,0:T(8,128)(2,1)S(1)} %get-tuple-element.33), channel_id=1, source_target_pairs={{0,224},{32,64},{64,32},{96,128},{128,96},{160,192},{192,160},{224... | collective-permute-start | bytes 589832 | tf_op jit(solution)/shard_map/ppermute | solution.py:96
  10.0 5.6 %collective-permute-start.2 = (bf16[24,16,256]{2,1,0:T(8,128)(2,1)S(1)}, bf16[24,16,256]{2,1,0:T(8,128)(2,1)S(1)}, u32[]{:S(2)}, u32[]{:S(2)}) collective-permute-start(bf16[24,16,256]{2,1,0:T(8,128)(2,1)S(1)} %get-tuple-element.31), channel_id=1, source_target_pairs={{0,32},{32,0},{64,96},{96,64},{128,160},{160,128},{192,224},{224,1... | collective-permute-start | bytes 589832 | tf_op jit(solution)/shard_map/ppermute | solution.py:99
  10.1 8.2 %collective-permute-start.3 = (bf16[24,16,256]{2,1,0:T(8,128)(2,1)S(1)}, bf16[24,16,256]{2,1,0:T(8,128)(2,1)S(1)}, u32[]{:S(2)}, u32[]{:S(2)}) collective-permute-start(bf16[24,16,256]{2,1,0:T(8,128)(2,1)S(1)} %get-tuple-element.36), channel_id=1, source_target_pairs={{0,224},{32,64},{64,32},{96,128},{128,96},{160,192},{192,160},{224... | collective-permute-start | bytes 589832 | tf_op jit(solution)/shard_map/ppermute | solution.py:99
  13.7 7.8 %collective-permute-start.5 = (bf16[24,16,256]{2,1,0:T(8,128)(2,1)S(1)}, bf16[24,16,256]{2,1,0:T(8,128)(2,1)S(1)}, u32[]{:S(2)}, u32[]{:S(2)}) collective-permute-start(bf16[24,16,256]{2,1,0:T(8,128)(2,1)S(1)} %add.216), channel_id=1, source_target_pairs={{0,224},{32,64},{64,32},{96,128},{128,96},{160,192},{192,160},{224... | collective-permute-start | bytes 589832 | tf_op jit(solution)/shard_map/ppermute | solution.py:114
  15.2 4.9 %collective-permute-start.4 = (bf16[24,16,256]{2,1,0:T(8,128)(2,1)S(1)}, bf16[24,16,256]{2,1,0:T(8,128)(2,1)S(1)}, u32[]{:S(2)}, u32[]{:S(2)}) collective-permute-start(bf16[24,16,256]{2,1,0:T(8,128)(2,1)S(1)} %add.217), channel_id=1, source_target_pairs={{0,32},{32,0},{64,96},{96,64},{128,160},{160,128},{192,224},{224,1... | collective-permute-start | bytes 589832 | tf_op jit(solution)/shard_map/ppermute | solution.py:114
  15.6 10.9 %collective-permute-start.7 = (bf16[24,16,256]{2,1,0:T(8,128)(2,1)S(1)}, bf16[24,16,256]{2,1,0:T(8,128)(2,1)S(1)}, u32[]{:S(2)}, u32[]{:S(2)}) collective-permute-start(bf16[24,16,256]{2,1,0:T(8,128)(2,1)S(1)} %add.218), channel_id=1, source_target_pairs={{0,224},{32,64},{64,32},{96,128},{128,96},{160,192},{192,160},{224... | collective-permute-start | bytes 589832 | tf_op jit(solution)/shard_map/ppermute | solution.py:114
  18.3 7.0 %collective-permute-start.6 = (bf16[24,16,256]{2,1,0:T(8,128)(2,1)S(1)}, bf16[24,16,256]{2,1,0:T(8,128)(2,1)S(1)}, u32[]{:S(2)}, u32[]{:S(2)}) collective-permute-start(bf16[24,16,256]{2,1,0:T(8,128)(2,1)S(1)} %add.219), channel_id=1, source_target_pairs={{0,32},{32,0},{64,96},{96,64},{128,160},{160,128},{192,224},{224,1... | collective-permute-start | bytes 589832 | tf_op jit(solution)/shard_map/ppermute | solution.py:114
  20.1 10.7 %collective-permute-start.9 = (bf16[24,16,256]{2,1,0:T(8,128)(2,1)S(1)}, bf16[24,16,256]{2,1,0:T(8,128)(2,1)S(1)}, u32[]{:S(2)}, u32[]{:S(2)}) collective-permute-start(bf16[24,16,256]{2,1,0:T(8,128)(2,1)S(1)} %add.220), channel_id=1, source_target_pairs={{0,224},{32,64},{64,32},{96,128},{128,96},{160,192},{192,160},{224... | collective-permute-start | bytes 589832 | tf_op jit(solution)/shard_map/ppermute | solution.py:114
  21.6 7.2 %collective-permute-start.8 = (bf16[24,16,256]{2,1,0:T(8,128)(2,1)S(1)}, bf16[24,16,256]{2,1,0:T(8,128)(2,1)S(1)}, u32[]{:S(2)}, u32[]{:S(2)}) collective-permute-start(bf16[24,16,256]{2,1,0:T(8,128)(2,1)S(1)} %add.221), channel_id=1, source_target_pairs={{0,32},{32,0},{64,96},{96,64},{128,160},{160,128},{192,224},{224,1... | collective-permute-start | bytes 589832 | tf_op jit(solution)/shard_map/ppermute | solution.py:114
  25.3 8.4 %collective-permute-start.10 = (bf16[24,16,256]{2,1,0:T(8,128)(2,1)S(1)}, bf16[24,16,256]{2,1,0:T(8,128)(2,1)S(1)}, u32[]{:S(2)}, u32[]{:S(2)}) collective-permute-start(bf16[24,16,256]{2,1,0:T(8,128)(2,1)S(1)} %add.222), channel_id=1, source_target_pairs={{0,224},{32,64},{64,32},{96,128},{128,96},{160,192},{192,160},{224... | collective-permute-start | bytes 589832 | tf_op jit(solution)/shard_map/ppermute | solution.py:114
  26.6 7.2 %collective-permute-start.11 = (bf16[24,16,256]{2,1,0:T(8,128)(2,1)S(1)}, bf16[24,16,256]{2,1,0:T(8,128)(2,1)S(1)}, u32[]{:S(2)}, u32[]{:S(2)}) collective-permute-start(bf16[24,16,256]{2,1,0:T(8,128)(2,1)S(1)} %add.223), channel_id=1, source_target_pairs={{0,32},{32,0},{64,96},{96,64},{128,160},{160,128},{192,224},{224,1... | collective-permute-start | bytes 589832 | tf_op jit(solution)/shard_map/ppermute | solution.py:114
  28.8 8.7 %collective-permute-start.13 = (bf16[24,16,256]{2,1,0:T(8,128)(2,1)S(1)}, bf16[24,16,256]{2,1,0:T(8,128)(2,1)S(1)}, u32[]{:S(2)}, u32[]{:S(2)}) collective-permute-start(bf16[24,16,256]{2,1,0:T(8,128)(2,1)S(1)} %add.224), channel_id=1, source_target_pairs={{0,224},{32,64},{64,32},{96,128},{128,96},{160,192},{192,160},{224... | collective-permute-start | bytes 589832 | tf_op jit(solution)/shard_map/ppermute | solution.py:114
  30.8 29.3 %copy-start = (bf16[1,1,512,512]{3,2,1,0:T(8,128)(2,1)S(1)}, bf16[1,1,512,512]{3,2,1,0:T(8,128)(2,1)}, u32[]{:S(2)}) copy-start(bf16[1,1,512,512]{3,2,1,0:T(8,128)(2,1)} %param.10) | copy-start | bytes 1572868
  30.8 29.3 %copy-start.1 = (bf16[1,1,512,512]{3,2,1,0:T(8,128)(2,1)S(1)}, bf16[1,1,512,512]{3,2,1,0:T(8,128)(2,1)}, u32[]{:S(2)}) copy-start(bf16[1,1,512,512]{3,2,1,0:T(8,128)(2,1)} %param.11) | copy-start | bytes 1572868
  30.8 7.0 %collective-permute-start.12 = (bf16[24,16,256]{2,1,0:T(8,128)(2,1)S(1)}, bf16[24,16,256]{2,1,0:T(8,128)(2,1)S(1)}, u32[]{:S(2)}, u32[]{:S(2)}) collective-permute-start(bf16[24,16,256]{2,1,0:T(8,128)(2,1)S(1)} %add.225), channel_id=1, source_target_pairs={{0,32},{32,0},{64,96},{96,64},{128,160},{160,128},{192,224},{224,1... | collective-permute-start | bytes 589832 | tf_op jit(solution)/shard_map/ppermute | solution.py:114
  37.8 28.0 %copy-start.2 = (f32[1,1,512,512]{3,2,1,0:T(8,128)S(1)}, f32[1,1,512,512]{3,2,1,0:T(8,128)}, u32[]{:S(2)}) copy-start(f32[1,1,512,512]{3,2,1,0:T(8,128)} %param.8) | copy-start | bytes 3145732
  62.0 15.2 %all-to-all-start.1 = ((bf16[32,16,512]{2,1,0:T(8,128)(2,1)}), bf16[32,16,512]{2,1,0:T(8,128)(2,1)S(1)}, u32[]{:S(2)}, u32[]{:S(2)}) async-start(bf16[32,16,512]{2,1,0:T(8,128)(2,1)} %bitcast.17), calls=%async_computation.1 | async-start | bytes 1048576 | tf_op jit(solution)/shard_map/all_to_all | solution.py:269

commit v4 on v2

--- a/solution.py
+++ b/solution.py
@@ -99,10 +99,8 @@
         for at, one, two in ((step, 0, 1), (step - 1, 1, 0)):
             if at == 0:
                 continue
-            for array, part, group, pairs in (
-                (down, one, me + at, back),
-                (up, two, me - at, ahead),
-            ):
+            sends = [(down, one, me + at, back), (up, two, me - at, ahead)]
+            for array, part, group, pairs in sends[::-1] if step == 1 else sends:
                 got = array[part]
                 if last is not None:
                     last, got = ordered(last, got)

time: 77.9 us -> 78.4 us (level)
  transfers between devices with their start and end apart: 15 -> 15, of which waited for: 6 -> 7; matrix products, arithmetic and copies ran while one was open for 9% -> 9% of each run, Pallas kernels for 2% -> 2%
where the time goes in v4:
time: 78.4 us; the launch traced here: 77.8 us
  starting transfers between devices  27.4 us (35%)
  blocking collectives  21.5 us (27%)
  waiting for transfers between devices  15 us (19%)
  Pallas kernels  6.09 us (8%)
  matrix products  4.13 us (5%)
  local copies, waits for them, and re-layouts  2.15 us (3%)
  between operations  1.05 us (1%)
    all_to_all x1, blocking collectives, local(): lax.all_to_all(sends, 'own', 0, 0, tiled=True).reshape(block_size, width)  21.5 us
    ppermute x10, starting transfers between devices, chains(): array[part] = lax.ppermute(last, 'rep', pairs)  14.4 us
    ppermute x10, waiting for transfers between devices, chains(): array[part] = lax.ppermute(last, 'rep', pairs)  7.55 us
    all_to_all x1, waiting for transfers between devices, local(): rows = lax.all_to_all(grafted, 'own', 0, 0, tiled=True)  7.45 us
    ppermute x2, starting transfers between devices, chains(): lax.ppermute(two, 'rep', ahead)  6.69 us
    all_to_all x1, starting transfers between devices, local(): rows = lax.all_to_all(grafted, 'own', 0, 0, tiled=True)  3.68 us
    dot_general x1, matrix products, local(): jnp.einsum('ki,kj->ij', block, block, preferred_element_type=jnp.float32)  2.67 us
    ppermute x2, starting transfers between devices, chains(): lax.ppermute(one, 'rep', back)  2.63 us
  transfers between devices with their start and end apart: 15, of which 7 were waited for; matrix products, arithmetic and copies ran while one was open for 9% of the time, Pallas kernels for 2%

profile of v4, /device:TPU:1, one launch (start us, length us, event | category | flops | bytes accessed | tf_op | source)
XLA Modules:
  0.0 77.8 jit_solution(15276146038893259985)
XLA Ops:
  0.6 1.1 %slices.2 = (bf16[24,16,256]{2,1,0:T(8,128)(2,1)S(1)}, bf16[24,16,256]{2,1,0:T(8,128)(2,1)S(1)}) custom-call(bf16[8,24,16,512]{3,2,1,0:T(8,128)(2,1)} %bitcast.47), custom_call_target="tpu_custom_call" | custom-call | bytes 1000000 | tf_op jit(solution)/shard_map/slices/pallas_call | solution.py:41
  1.7 2.5 %collective-permute-start = (bf16[24,16,256]{2,1,0:T(8,128)(2,1)S(1)}, bf16[24,16,256]{2,1,0:T(8,128)(2,1)S(1)}, u32[]{:S(2)}, u32[]{:S(2)}) collective-permute-start(bf16[24,16,256]{2,1,0:T(8,128)(2,1)S(1)} %get-tuple-element.29), channel_id=1, source_target_pairs={{0,32},{32,64},{64,96},{96,128},{128,160},{160,192},{192,224},{224... | collective-permute-start | bytes 589832 | tf_op jit(solution)/shard_map/ppermute | solution.py:92
  4.2 4.0 %collective-permute-start.1 = (bf16[24,16,256]{2,1,0:T(8,128)(2,1)S(1)}, bf16[24,16,256]{2,1,0:T(8,128)(2,1)S(1)}, u32[]{:S(2)}, u32[]{:S(2)}) collective-permute-start(bf16[24,16,256]{2,1,0:T(8,128)(2,1)S(1)} %get-tuple-element.33), channel_id=1, source_target_pairs={{0,224},{32,0},{64,32},{96,64},{128,96},{160,128},{192,160},{224,1... | collective-permute-start | bytes 589832 | tf_op jit(solution)/shard_map/ppermute | solution.py:92
  8.3 1.0 %slices.3 = (bf16[24,16,256]{2,1,0:T(8,128)(2,1)S(1)}, bf16[24,16,256]{2,1,0:T(8,128)(2,1)S(1)}) custom-call(bf16[8,24,16,512]{3,2,1,0:T(8,128)(2,1)} %bitcast.48), custom_call_target="tpu_custom_call" | custom-call | bytes 1000000 | tf_op jit(solution)/shard_map/slices/pallas_call | solution.py:41
  9.3 0.1 collective-permute-start.2
  9.4 2.7 %collective-permute-start.3 = (bf16[24,16,256]{2,1,0:T(8,128)(2,1)S(1)}, bf16[24,16,256]{2,1,0:T(8,128)(2,1)S(1)}, u32[]{:S(2)}, u32[]{:S(2)}) collective-permute-start(bf16[24,16,256]{2,1,0:T(8,128)(2,1)S(1)} %get-tuple-element.36), channel_id=1, source_target_pairs={{0,224},{32,0},{64,32},{96,64},{128,96},{160,128},{192,160},{224,1... | collective-permute-start | bytes 589832 | tf_op jit(solution)/shard_map/ppermute | solution.py:95
  12.1 0.1 broadcast_in_dim.6
  12.2 0.1 eq.74
  12.2 2.0 %dynamic-slice_bitcast_fusion = (bf16[24,16,512]{2,1,0:T(8,128)(2,1)S(1)}, bf16[24,16,512]{2,1,0:T(8,128)(2,1)S(1)}, bf16[24,16,512]{2,1,0:T(8,128)(2,1)S(1)}, b...) fusion(bf16[8,24,16,512]{3,2,1,0:T(8,128)(2,1)} %bitcast.49, ...), kind=kLoop, calls=%fused_computation.9 | loop fusion | bytes 5505052 | tf_op jit(solution)/shard_map/jit(dynamic_index_in_dim)/squeeze | solution.py:88
  14.2 0.0 collective-permute-done.got_ref
  14.3 0.1 collective-permute-start.4
  14.4 0.0 collective-permute-done.1.got_ref
  14.4 2.7 %collective-permute-start.5 = (bf16[24,16,256]{2,1,0:T(8,128)(2,1)S(1)}, bf16[24,16,256]{2,1,0:T(8,128)(2,1)S(1)}, u32[]{:S(2)}, u32[]{:S(2)}) collective-permute-start(bf16[24,16,256]{2,1,0:T(8,128)(2,1)S(1)} %add.205), channel_id=1, source_target_pairs={{0,224},{32,0},{64,32},{96,64},{128,96},{160,128},{192,160},{224,1... | collective-permute-start | bytes 589832 | tf_op jit(solution)/shard_map/ppermute | solution.py:110
  17.1 0.2 and_convert_fusion.take_ref
  17.3 0.0 collective-permute-done.2.got_ref
  17.4 0.1 collective-permute-start.6
  17.4 0.0 collective-permute-done.3.got_ref
  17.5 2.7 %collective-permute-start.7 = (bf16[24,16,256]{2,1,0:T(8,128)(2,1)S(1)}, bf16[24,16,256]{2,1,0:T(8,128)(2,1)S(1)}, u32[]{:S(2)}, u32[]{:S(2)}) collective-permute-start(bf16[24,16,256]{2,1,0:T(8,128)(2,1)S(1)} %add.207), channel_id=1, source_target_pairs={{0,224},{32,0},{64,32},{96,64},{128,96},{160,128},{192,160},{224,1... | collective-permute-start | bytes 589832 | tf_op jit(solution)/shard_map/ppermute | solution.py:110
  20.2 0.2 collective-permute-done.4.got_ref
  20.5 0.1 collective-permute-start.9
  20.5 0.0 collective-permute-done.5.got_ref
  20.6 2.7 %collective-permute-start.8 = (bf16[24,16,256]{2,1,0:T(8,128)(2,1)S(1)}, bf16[24,16,256]{2,1,0:T(8,128)(2,1)S(1)}, u32[]{:S(2)}, u32[]{:S(2)}) collective-permute-start(bf16[24,16,256]{2,1,0:T(8,128)(2,1)S(1)} %add.209), channel_id=1, source_target_pairs={{0,224},{32,0},{64,32},{96,64},{128,96},{160,128},{192,160},{224,1... | collective-permute-start | bytes 589832 | tf_op jit(solution)/shard_map/ppermute | solution.py:110
  23.3 0.2 and_convert_fusion.1.put_ref
  23.5 1.7 %collective-permute-done.6.got_ref = bf16[24,16,256]{2,1,0:T(8,128)(2,1)S(1)} collective-permute-done((bf16[24,16,256]{2,1,0:T(8,128)(2,1)S(1)}, bf16[24,16,256]{2,1,0:T(8,128)(2,1)S(1)}, u32[]{:S(2)}, u32[]{:S(2)}) %collective-permute-start.6) | collective-permute-done | bytes 196640 | tf_op jit(solution)/shard_map/ppermute | solution.py:110
  25.2 0.1 collective-permute-start.10
  25.3 0.0 collective-permute-done.7.got_ref
  25.4 2.8 %collective-permute-start.11 = (bf16[24,16,256]{2,1,0:T(8,128)(2,1)S(1)}, bf16[24,16,256]{2,1,0:T(8,128)(2,1)S(1)}, u32[]{:S(2)}, u32[]{:S(2)}) collective-permute-start(bf16[24,16,256]{2,1,0:T(8,128)(2,1)S(1)} %add.211), channel_id=1, source_target_pairs={{0,224},{32,0},{64,32},{96,64},{128,96},{160,128},{192,160},{224,1... | collective-permute-start | bytes 589832 | tf_op jit(solution)/shard_map/ppermute | solution.py:110
  28.1 0.2 collective-permute-done.8.got_ref
  28.4 0.7 collective-permute-done.9.got_ref
  29.1 0.0 copy-start
  29.1 0.0 copy-start.1
  29.1 0.1 collective-permute-start.13
  29.2 3.0 %collective-permute-start.12 = (bf16[24,16,256]{2,1,0:T(8,128)(2,1)S(1)}, bf16[24,16,256]{2,1,0:T(8,128)(2,1)S(1)}, u32[]{:S(2)}, u32[]{:S(2)}) collective-permute-start(bf16[24,16,256]{2,1,0:T(8,128)(2,1)S(1)} %add.212), channel_id=1, source_target_pairs={{0,224},{32,0},{64,32},{96,64},{128,96},{160,128},{192,160},{224,1... | collective-permute-start | bytes 589832 | tf_op jit(solution)/shard_map/ppermute | solution.py:110
  32.2 0.5 collective-permute-done.10.down_ref
  32.8 0.0 collective-permute-done.11.down_ref
  32.8 0.1 widen.3.wide_ref
  32.8 4.3 %collective-permute-done.13.got_ref = bf16[24,16,256]{2,1,0:T(8,128)(2,1)S(1)} collective-permute-done((bf16[24,16,256]{2,1,0:T(8,128)(2,1)S(1)}, bf16[24,16,256]{2,1,0:T(8,128)(2,1)S(1)}, u32[]{:S(2)}, u32[]{:S(2)}) %collective-permute-start.13) | collective-permute-done | bytes 196640 | tf_op jit(solution)/shard_map/ppermute | solution.py:110
  37.1 0.3 place.2.refs_0_
  37.4 0.0 copy-start.2
  37.4 0.0 collective-permute-done.12.got_ref
  37.4 0.3 place.3
  37.7 21.5 %all_to_all.10 = bf16[32,16,512]{2,1,0:T(8,128)(2,1)S(1)} all-to-all(bf16[32,16,512]{2,1,0:T(8,128)(2,1)S(1)} %bitcast.43), channel_id=1, replica_groups=mesh['rep'=8,'own'=32] {'own'}, dimensions={0} | all-to-all | bytes 1048576 | tf_op jit(solution)/shard_map/all_to_all | solution.py:258
  59.3 1.9 %graft.1 = bf16[512,512]{1,0:T(8,128)(2,1)} custom-call(bf16[512,512]{1,0:T(8,128)(2,1)S(1)} %bitcast.41, bf16[512,512]{1,0:T(8,128)(2,1)S(1)} %bitcast.45, bf16[512,512]{1,0:T(8,128)(2,1)S(1)} %bitcast.46), custom_call_target="tpu_custom_call" | custom-call | flops 536870912 | bytes 2097152 | tf_op jit(solution)/shard_map/graft/pallas_call | solution.py:195
  61.2 3.7 %all-to-all-start.1 = ((bf16[32,16,512]{2,1,0:T(8,128)(2,1)}), bf16[32,16,512]{2,1,0:T(8,128)(2,1)S(1)}, u32[]{:S(2)}, u32[]{:S(2)}) async-start(bf16[32,16,512]{2,1,0:T(8,128)(2,1)} %bitcast.17), calls=%async_computation.1 | async-start | bytes 1048576 | tf_op jit(solution)/shard_map/all_to_all | solution.py:261
  64.9 1.5 %fusion.2 = f32[1,1,512,512]{3,2,1,0:T(8,128)} fusion(bf16[512,512]{1,0:T(8,128)(2,1)S(1)} %bitcast.42, f32[1,1,512,512]{3,2,1,0:T(8,128)S(1)} %copy-done.2), kind=kOutput, calls=%fused_computation.4 | convolution fusion | flops 269221888 | bytes 2621440 | tf_op jit(solution)/shard_map/ik,jk->ij/dot_general | solution.py:263
  66.3 2.7 %fusion.4 = f32[1,1,512,512]{3,2,1,0:T(8,128)} fusion(bf16[32,16,512]{2,1,0:T(8,128)(2,1)S(1)} %all_to_all.10, f32[1,1,512,512]{3,2,1,0:T(8,128)} %param.9), kind=kOutput, calls=%fused_computation.6 | convolution fusion | flops 269221888 | bytes 2621440 | tf_op jit(solution)/shard_map/ki,kj->ij/dot_general | solution.py:264
  69.0 7.4 %all-to-all-done.1 = bf16[32,16,512]{2,1,0:T(8,128)(2,1)S(1)} async-done(((bf16[32,16,512]{2,1,0:T(8,128)(2,1)}), bf16[32,16,512]{2,1,0:T(8,128)(2,1)S(1)}, u32[]{:S(2)}, u32[]{:S(2)}) %all-to-all-start.1) | async-done | bytes 524320 | tf_op jit(solution)/shard_map/all_to_all | solution.py:261
  76.5 1.1 %pick.1 = f32[24,16,512]{2,1,0:T(8,128)} custom-call(bf16[384,512]{1,0:T(8,128)(2,1)S(1)} %and_convert_fusion.take_ref, bf16[512,512]{1,0:T(8,128)(2,1)S(1)} %bitcast.44), custom_call_target="tpu_custom_call" | custom-call | bytes 1300000 | tf_op jit(solution)/shard_map/pick/pallas_call | solution.py:231
  (18 shorter events, 0.3 us)
Async XLA Ops:
  0.6 11.5 %copy-start.3 = (s32[24]{0:T(128)S(1)}, s32[24]{0:T(128)}, u32[]{:S(2)}) copy-start(s32[24]{0:T(128)} %param.7) | copy-start | bytes 292
  1.7 12.5 %collective-permute-start = (bf16[24,16,256]{2,1,0:T(8,128)(2,1)S(1)}, bf16[24,16,256]{2,1,0:T(8,128)(2,1)S(1)}, u32[]{:S(2)}, u32[]{:S(2)}) collective-permute-start(bf16[24,16,256]{2,1,0:T(8,128)(2,1)S(1)} %get-tuple-element.29), channel_id=1, source_target_pairs={{0,32},{32,64},{64,96},{96,128},{128,160},{160,192},{192,224},{224... | collective-permute-start | bytes 589832 | tf_op jit(solution)/shard_map/ppermute | solution.py:92
  4.2 10.1 %collective-permute-start.1 = (bf16[24,16,256]{2,1,0:T(8,128)(2,1)S(1)}, bf16[24,16,256]{2,1,0:T(8,128)(2,1)S(1)}, u32[]{:S(2)}, u32[]{:S(2)}) collective-permute-start(bf16[24,16,256]{2,1,0:T(8,128)(2,1)S(1)} %get-tuple-element.33), channel_id=1, source_target_pairs={{0,224},{32,0},{64,32},{96,64},{128,96},{160,128},{192,160},{224,1... | collective-permute-start | bytes 589832 | tf_op jit(solution)/shard_map/ppermute | solution.py:92
  9.3 8.0 %collective-permute-start.2 = (bf16[24,16,256]{2,1,0:T(8,128)(2,1)S(1)}, bf16[24,16,256]{2,1,0:T(8,128)(2,1)S(1)}, u32[]{:S(2)}, u32[]{:S(2)}) collective-permute-start(bf16[24,16,256]{2,1,0:T(8,128)(2,1)S(1)} %get-tuple-element.31), channel_id=1, source_target_pairs={{0,32},{32,64},{64,96},{96,128},{128,160},{160,192},{192,224},{224... | collective-permute-start | bytes 589832 | tf_op jit(solution)/shard_map/ppermute | solution.py:95
  9.4 8.0 %collective-permute-start.3 = (bf16[24,16,256]{2,1,0:T(8,128)(2,1)S(1)}, bf16[24,16,256]{2,1,0:T(8,128)(2,1)S(1)}, u32[]{:S(2)}, u32[]{:S(2)}) collective-permute-start(bf16[24,16,256]{2,1,0:T(8,128)(2,1)S(1)} %get-tuple-element.36), channel_id=1, source_target_pairs={{0,224},{32,0},{64,32},{96,64},{128,96},{160,128},{192,160},{224,1... | collective-permute-start | bytes 589832 | tf_op jit(solution)/shard_map/ppermute | solution.py:95
  14.3 6.2 %collective-permute-start.4 = (bf16[24,16,256]{2,1,0:T(8,128)(2,1)S(1)}, bf16[24,16,256]{2,1,0:T(8,128)(2,1)S(1)}, u32[]{:S(2)}, u32[]{:S(2)}) collective-permute-start(bf16[24,16,256]{2,1,0:T(8,128)(2,1)S(1)} %add.204), channel_id=1, source_target_pairs={{0,32},{32,64},{64,96},{96,128},{128,160},{160,192},{192,224},{224... | collective-permute-start | bytes 589832 | tf_op jit(solution)/shard_map/ppermute | solution.py:110
  14.4 6.2 %collective-permute-start.5 = (bf16[24,16,256]{2,1,0:T(8,128)(2,1)S(1)}, bf16[24,16,256]{2,1,0:T(8,128)(2,1)S(1)}, u32[]{:S(2)}, u32[]{:S(2)}) collective-permute-start(bf16[24,16,256]{2,1,0:T(8,128)(2,1)S(1)} %add.205), channel_id=1, source_target_pairs={{0,224},{32,0},{64,32},{96,64},{128,96},{160,128},{192,160},{224,1... | collective-permute-start | bytes 589832 | tf_op jit(solution)/shard_map/ppermute | solution.py:110
  17.4 7.8 %collective-permute-start.6 = (bf16[24,16,256]{2,1,0:T(8,128)(2,1)S(1)}, bf16[24,16,256]{2,1,0:T(8,128)(2,1)S(1)}, u32[]{:S(2)}, u32[]{:S(2)}) collective-permute-start(bf16[24,16,256]{2,1,0:T(8,128)(2,1)S(1)} %add.206), channel_id=1, source_target_pairs={{0,32},{32,64},{64,96},{96,128},{128,160},{160,192},{192,224},{224... | collective-permute-start | bytes 589832 | tf_op jit(solution)/shard_map/ppermute | solution.py:110
  17.5 7.8 %collective-permute-start.7 = (bf16[24,16,256]{2,1,0:T(8,128)(2,1)S(1)}, bf16[24,16,256]{2,1,0:T(8,128)(2,1)S(1)}, u32[]{:S(2)}, u32[]{:S(2)}) collective-permute-start(bf16[24,16,256]{2,1,0:T(8,128)(2,1)S(1)} %add.207), channel_id=1, source_target_pairs={{0,224},{32,0},{64,32},{96,64},{128,96},{160,128},{192,160},{224,1... | collective-permute-start | bytes 589832 | tf_op jit(solution)/shard_map/ppermute | solution.py:110
  20.5 8.6 %collective-permute-start.9 = (bf16[24,16,256]{2,1,0:T(8,128)(2,1)S(1)}, bf16[24,16,256]{2,1,0:T(8,128)(2,1)S(1)}, u32[]{:S(2)}, u32[]{:S(2)}) collective-permute-start(bf16[24,16,256]{2,1,0:T(8,128)(2,1)S(1)} %add.208), channel_id=1, source_target_pairs={{0,32},{32,64},{64,96},{96,128},{128,160},{160,192},{192,224},{224... | collective-permute-start | bytes 589832 | tf_op jit(solution)/shard_map/ppermute | solution.py:110
  20.6 7.7 %collective-permute-start.8 = (bf16[24,16,256]{2,1,0:T(8,128)(2,1)S(1)}, bf16[24,16,256]{2,1,0:T(8,128)(2,1)S(1)}, u32[]{:S(2)}, u32[]{:S(2)}) collective-permute-start(bf16[24,16,256]{2,1,0:T(8,128)(2,1)S(1)} %add.209), channel_id=1, source_target_pairs={{0,224},{32,0},{64,32},{96,64},{128,96},{160,128},{192,160},{224,1... | collective-permute-start | bytes 589832 | tf_op jit(solution)/shard_map/ppermute | solution.py:110
  25.2 7.5 %collective-permute-start.10 = (bf16[24,16,256]{2,1,0:T(8,128)(2,1)S(1)}, bf16[24,16,256]{2,1,0:T(8,128)(2,1)S(1)}, u32[]{:S(2)}, u32[]{:S(2)}) collective-permute-start(bf16[24,16,256]{2,1,0:T(8,128)(2,1)S(1)} %add.210), channel_id=1, source_target_pairs={{0,32},{32,64},{64,96},{96,128},{128,160},{160,192},{192,224},{224... | collective-permute-start | bytes 589832 | tf_op jit(solution)/shard_map/ppermute | solution.py:110
  25.4 7.4 %collective-permute-start.11 = (bf16[24,16,256]{2,1,0:T(8,128)(2,1)S(1)}, bf16[24,16,256]{2,1,0:T(8,128)(2,1)S(1)}, u32[]{:S(2)}, u32[]{:S(2)}) collective-permute-start(bf16[24,16,256]{2,1,0:T(8,128)(2,1)S(1)} %add.211), channel_id=1, source_target_pairs={{0,224},{32,0},{64,32},{96,64},{128,96},{160,128},{192,160},{224,1... | collective-permute-start | bytes 589832 | tf_op jit(solution)/shard_map/ppermute | solution.py:110
  29.1 30.2 %copy-start = (bf16[1,1,512,512]{3,2,1,0:T(8,128)(2,1)S(1)}, bf16[1,1,512,512]{3,2,1,0:T(8,128)(2,1)}, u32[]{:S(2)}) copy-start(bf16[1,1,512,512]{3,2,1,0:T(8,128)(2,1)} %param.10) | copy-start | bytes 1572868
  29.1 30.2 %copy-start.1 = (bf16[1,1,512,512]{3,2,1,0:T(8,128)(2,1)S(1)}, bf16[1,1,512,512]{3,2,1,0:T(8,128)(2,1)}, u32[]{:S(2)}) copy-start(bf16[1,1,512,512]{3,2,1,0:T(8,128)(2,1)} %param.11) | copy-start | bytes 1572868
  29.1 8.0 %collective-permute-start.13 = (bf16[24,16,256]{2,1,0:T(8,128)(2,1)S(1)}, bf16[24,16,256]{2,1,0:T(8,128)(2,1)S(1)}, u32[]{:S(2)}, u32[]{:S(2)}) collective-permute-start(bf16[24,16,256]{2,1,0:T(8,128)(2,1)S(1)} %add.213), channel_id=1, source_target_pairs={{0,32},{32,64},{64,96},{96,128},{128,160},{160,192},{192,224},{224... | collective-permute-start | bytes 589832 | tf_op jit(solution)/shard_map/ppermute | solution.py:110
  29.2 8.2 %collective-permute-start.12 = (bf16[24,16,256]{2,1,0:T(8,128)(2,1)S(1)}, bf16[24,16,256]{2,1,0:T(8,128)(2,1)S(1)}, u32[]{:S(2)}, u32[]{:S(2)}) collective-permute-start(bf16[24,16,256]{2,1,0:T(8,128)(2,1)S(1)} %add.212), channel_id=1, source_target_pairs={{0,224},{32,0},{64,32},{96,64},{128,96},{160,128},{192,160},{224,1... | collective-permute-start | bytes 589832 | tf_op jit(solution)/shard_map/ppermute | solution.py:110
  37.4 27.5 %copy-start.2 = (f32[1,1,512,512]{3,2,1,0:T(8,128)S(1)}, f32[1,1,512,512]{3,2,1,0:T(8,128)}, u32[]{:S(2)}) copy-start(f32[1,1,512,512]{3,2,1,0:T(8,128)} %param.8) | copy-start | bytes 3145732
  61.2 15.3 %all-to-all-start.1 = ((bf16[32,16,512]{2,1,0:T(8,128)(2,1)}), bf16[32,16,512]{2,1,0:T(8,128)(2,1)S(1)}, u32[]{:S(2)}, u32[]{:S(2)}) async-start(bf16[32,16,512]{2,1,0:T(8,128)(2,1)} %bitcast.17), calls=%async_computation.1 | async-start | bytes 1048576 | tf_op jit(solution)/shard_map/all_to_all | solution.py:261
